TPU v7x, 512 devices: a whole 4x4x16 slice. The times are simulated.
512 devices in a mesh: seq: 32 (over x, y, core), batch: 16 (over z).
Axes of the slice: x: 4, y: 4, z: 16, core: 2. Of those that a mesh axis runs over, the one named last changes fastest.
Arguments:
- queries: bfloat16 [16, 16384, 256], P('batch', 'seq'), may hold values from -6 to 6
- key_rows: bfloat16 [16, 16384, 256], P('batch', 'seq'), may hold values from -6 to 6
- value_rows: bfloat16 [16, 16384, 256], P('batch', 'seq'), may hold values from -6 to 6
- step_rates: float32 [16, 16384], P('batch', 'seq'), may hold values from 0.02 to 0.2
- cotangent: bfloat16 [16, 16384, 256], P('batch', 'seq'), may hold values from -0.01171875 to 0.01171875
- fast_init: float32 [768, 256], P('batch'), may hold values from -0.375 to 0.375
Outputs:
- layer_out: bfloat16 [16, 16384, 256], P('batch', 'seq')
- init_grad: float32 [768, 256], P('batch')
All inputs are finite; a program needn't handle non-finite values.
Results may differ from a plain program's by a relative error of at most 0.0012.
Values sent between devices are 32-bit elements; how exact they have to be, the bound alone decides.
A program may use at most 64 MiB of HBM per device.

v0:
```python
from functools import partial
import math

import jax
import jax.numpy as jnp
from jax import lax
from jax.sharding import Mesh
from jax.sharding import PartitionSpec as P

SEQ = ("seq_0", "seq_1", "seq_2")


def in_order(blocks, dim):
    blocks = jnp.moveaxis(blocks, 0, dim)
    shape = blocks.shape
    return blocks.reshape(*shape[:dim], shape[dim] * shape[dim + 1], *shape[dim + 2 :])


def from_everyone(value, axis):
    copies = jnp.broadcast_to(value, (lax.axis_size(axis), *value.shape))
    return lax.all_to_all(copies, axis, split_axis=0, concat_axis=0, tiled=True)


def gather_directly(value, axis, dim):
    return in_order(from_everyone(value, axis), dim)


def rows_for(lines, peers):
    spare = -lines.shape[0] % peers
    if not spare:
        return lines
    return jnp.concatenate([lines, jnp.zeros((spare, *lines.shape[1:]), lines.dtype)])


def gathered_by_axis(value, axes, dim):
    far, near = axes
    first = from_everyone(value, far)
    blocks = jnp.swapaxes(from_everyone(first, near), 0, 1)
    return in_order(blocks.reshape(-1, *value.shape), dim)


def in_blocks(value, dim, peers):
    before, after = (value.shape[:dim], value.shape[dim + 1 :])
    return jnp.moveaxis(value.reshape(*before, peers, -1, *after), dim, 0)


def sum_at_owner(value, axis, dim):
    peers = lax.axis_size(axis)
    blocks = lax.all_to_all(in_blocks(value, dim, peers), axis, 0, 0, tiled=True)
    return jnp.sum(blocks, axis=0)


def summed_rows(value, axes, dim):
    far, near = axes
    blocks = in_blocks(value, dim, lax.axis_size(far))
    nearer = sum_at_owner(blocks, near, dim + 1)
    arrived = lax.all_to_all(nearer, far, split_axis=0, concat_axis=0, tiled=True)
    return arrived.sum(axis=0)


def sum_by_parts(value, axes):
    lines = value.reshape(-1, value.shape[-1])
    padded = rows_for(lines, lax.axis_size(axes[0]) * lax.axis_size(axes[1]))
    whole = gathered_by_axis(summed_rows(padded, axes, 0), axes, 0)
    return lax.slice_in_dim(whole, 0, len(lines)).reshape(value.shape)


def over_copies(value, axis):
    everything = from_everyone(value, axis)
    return jnp.sum(everything, axis=0)


def swiglu_apply(weights, row_block):
    high = lax.Precision.HIGHEST
    projected = jnp.dot(row_block, weights[0], precision=high, preferred_element_type=jnp.float32)
    gate_pre = jnp.dot(row_block, weights[1], precision=high, preferred_element_type=jnp.float32)
    hidden = jax.nn.silu(gate_pre) * projected
    return jnp.dot(hidden, weights[2].T, precision=high, preferred_element_type=jnp.float32)


def inner_loss(weights, key_block, value_block, scaled):
    return -jnp.sum(scaled[:, None] * swiglu_apply(weights, key_block) * value_block)


def inner_grad(weights, key_block, value_block, scaled):
    return jax.grad(inner_loss)(weights, key_block, value_block, scaled)


def body(queries, key_rows, value_rows, step_rates, cotangent, fast_init):
    width = queries.shape[2]
    hidden_units = fast_init.shape[1]
    shards = lax.axis_size(SEQ)
    divisor = math.sqrt(shards * queries.shape[1])
    query_block = queries[0].astype(jnp.float32)
    key_block = key_rows[0].astype(jnp.float32)
    value_block = value_rows[0].astype(jnp.float32)
    scaled = step_rates[0] / divisor
    cot_block = cotangent[0].astype(jnp.float32)
    gathered = gather_directly(fast_init, "batch", 0)
    initial = gathered.reshape(3, width, hidden_units)
    local_grad = partial(inner_grad, key_block=key_block, value_block=value_block, scaled=scaled)
    middle = initial - sum_by_parts(local_grad(initial), (("seq_0", "seq_1"), "seq_2"))
    final = middle - sum_by_parts(local_grad(middle), (("seq_0", "seq_1"), "seq_2"))
    result, pull_out = jax.vjp(partial(swiglu_apply, row_block=query_block), final)
    adjoint_two = sum_by_parts(pull_out(cot_block)[0], (("seq_0", "seq_1"), "seq_2"))
    _, pull_middle = jax.vjp(local_grad, middle)
    adjoint_one = adjoint_two - sum_by_parts(
        pull_middle(adjoint_two)[0], (("seq_0", "seq_1"), "seq_2")
    )
    _, pull_first = jax.vjp(local_grad, initial)
    local_term = pull_first(adjoint_one)[0].reshape(3 * width, hidden_units)
    adjoint_flat = adjoint_one.reshape(3 * width, hidden_units)
    combined = adjoint_flat * (1.0 / shards) - local_term
    summed = sum_at_owner(combined, "batch", 0)
    summed = over_copies(summed, SEQ)
    return (result.astype(jnp.bfloat16)[None], summed)


def solution(mesh):
    torus = Mesh(
        mesh.devices.reshape(4, 4, 2, mesh.shape["batch"]), ("seq_0", "seq_1", "seq_2", "batch")
    )
    return jax.shard_map(
        body,
        mesh=torus,
        in_specs=(
            P("batch", SEQ, None),
            P("batch", SEQ, None),
            P("batch", SEQ, None),
            P("batch", SEQ),
            P("batch", SEQ, None),
            P("batch", None),
        ),
        out_specs=(P("batch", SEQ, None), P("batch", None)),
        check_vma=False,
    )
```

profile of v0, /device:TPU:1, one launch (start us, length us, event | category | flops | bytes accessed | tf_op | source)
XLA Modules:
  0.0 304.6 jit_solution(10464993558258745897)
XLA Ops:
  0.7 1.8 broadcast_in_dim.86
  2.5 15.7 %all-to-all-start = ((f32[16,48,256]{2,1,0:T(8,128)}), f32[16,48,256]{2,1,0:T(8,128)S(1)}, u32[]{:S(2)}, u32[]{:S(2)}) async-start(f32[16,48,256]{2,1,0:T(8,128)} %broadcast_in_dim.86), calls=%async_computation | async-start | bytes 1572864 | tf_op jit(solution)/shard_map/all_to_all | solution.py:21
  18.3 34.5 %all-to-all-done = f32[16,48,256]{2,1,0:T(8,128)S(1)} async-done(((f32[16,48,256]{2,1,0:T(8,128)}), f32[16,48,256]{2,1,0:T(8,128)S(1)}, u32[]{:S(2)}, u32[]{:S(2)}) %all-to-all-start) | async-done | bytes 786464 | tf_op jit(solution)/shard_map/all_to_all | solution.py:21
  53.2 0.6 fusion.14
  54.2 0.6 convolution_bitcast_fusion.21
  54.8 1.1 convolution_bitcast_fusion.23
  55.9 0.6 convolution_bitcast_fusion.22
  56.7 9.8 %all_to_all.95 = f32[2,16,24,256]{3,2,1,0:T(8,128)S(1)} all-to-all(f32[2,16,24,256]{3,2,1,0:T(8,128)S(1)} %bitcast.236), channel_id=1, replica_groups=mesh['seq_0'=4,'seq_1'=4,'seq_2'=2,'batch'=16] {'seq_2'}, dimensions={0} | all-to-all | bytes 1572864 | tf_op jit(solution)/shard_map/all_to_all | solution.py:49
  66.5 15.8 %all_to_all.96 = f32[16,24,256]{2,1,0:T(8,128)S(1)} all-to-all(f32[16,24,256]{2,1,0:T(8,128)S(1)} %reduce_sum.107), channel_id=1, replica_groups=mesh['seq_0'=4,'seq_1'=4,'seq_2'=2,'batch'=16] {'seq_0','seq_1'}, dimensions={0} | all-to-all | bytes 786432 | tf_op jit(solution)/shard_map/all_to_all | solution.py:57
  82.4 11.2 %all_to_all.97 = f32[16,24,256]{2,1,0:T(8,128)S(1)} all-to-all(f32[16,24,256]{2,1,0:T(8,128)S(1)} %broadcast_in_dim.90), channel_id=1, replica_groups=mesh['seq_0'=4,'seq_1'=4,'seq_2'=2,'batch'=16] {'seq_0','seq_1'}, dimensions={0} | all-to-all | bytes 786432 | tf_op jit(solution)/shard_map/all_to_all | solution.py:21
  93.7 6.9 %all_to_all.98 = f32[2,16,24,256]{3,2,1,0:T(8,128)S(1)} all-to-all(f32[2,16,24,256]{3,2,1,0:T(8,128)S(1)} %broadcast_in_dim.91), channel_id=1, replica_groups=mesh['seq_0'=4,'seq_1'=4,'seq_2'=2,'batch'=16] {'seq_2'}, dimensions={0} | all-to-all | bytes 1572864 | tf_op jit(solution)/shard_map/all_to_all | solution.py:21
  100.8 0.6 fusion.12
  101.8 0.4 fusion.141
  102.3 0.6 convolution_bitcast_fusion.18
  102.9 1.1 convolution_bitcast_fusion.20
  104.0 0.6 convolution_bitcast_fusion.19
  104.8 4.4 %all_to_all.99 = f32[2,16,24,256]{3,2,1,0:T(8,128)S(1)} all-to-all(f32[2,16,24,256]{3,2,1,0:T(8,128)S(1)} %bitcast.237), channel_id=1, replica_groups=mesh['seq_0'=4,'seq_1'=4,'seq_2'=2,'batch'=16] {'seq_2'}, dimensions={0} | all-to-all | bytes 1572864 | tf_op jit(solution)/shard_map/all_to_all | solution.py:49
  109.1 0.8 reduce_sum.128
  109.9 12.8 %all_to_all.100 = f32[16,24,256]{2,1,0:T(8,128)S(1)} all-to-all(f32[16,24,256]{2,1,0:T(8,128)} %reduce_sum.128), channel_id=1, replica_groups=mesh['seq_0'=4,'seq_1'=4,'seq_2'=2,'batch'=16] {'seq_0','seq_1'}, dimensions={0} | all-to-all | bytes 786432 | tf_op jit(solution)/shard_map/all_to_all | solution.py:57
  122.8 11.4 %all_to_all.101 = f32[16,24,256]{2,1,0:T(8,128)S(1)} all-to-all(f32[16,24,256]{2,1,0:T(8,128)S(1)} %broadcast_in_dim.95), channel_id=1, replica_groups=mesh['seq_0'=4,'seq_1'=4,'seq_2'=2,'batch'=16] {'seq_0','seq_1'}, dimensions={0} | all-to-all | bytes 786432 | tf_op jit(solution)/shard_map/all_to_all | solution.py:21
  134.2 6.8 %all_to_all.102 = f32[2,16,24,256]{3,2,1,0:T(8,128)S(1)} all-to-all(f32[2,16,24,256]{3,2,1,0:T(8,128)S(1)} %broadcast_in_dim.96), channel_id=1, replica_groups=mesh['seq_0'=4,'seq_1'=4,'seq_2'=2,'batch'=16] {'seq_2'}, dimensions={0} | all-to-all | bytes 1572864 | tf_op jit(solution)/shard_map/all_to_all | solution.py:21
  141.3 0.8 copy-done.7
  143.6 0.6 convolution_bitcast_fusion.17
  144.2 0.7 convolution_bitcast_fusion.16
  144.9 0.6 convolution_bitcast_fusion.15
  145.6 4.3 %all_to_all.103 = f32[2,16,24,256]{3,2,1,0:T(8,128)S(1)} all-to-all(f32[2,16,24,256]{3,2,1,0:T(8,128)S(1)} %bitcast.238), channel_id=1, replica_groups=mesh['seq_0'=4,'seq_1'=4,'seq_2'=2,'batch'=16] {'seq_2'}, dimensions={0} | all-to-all | bytes 1572864 | tf_op jit(solution)/shard_map/all_to_all | solution.py:49
  150.0 12.5 %all_to_all.104 = f32[16,24,256]{2,1,0:T(8,128)S(1)} all-to-all(f32[16,24,256]{2,1,0:T(8,128)S(1)} %reduce_sum.130), channel_id=1, replica_groups=mesh['seq_0'=4,'seq_1'=4,'seq_2'=2,'batch'=16] {'seq_0','seq_1'}, dimensions={0} | all-to-all | bytes 786432 | tf_op jit(solution)/shard_map/all_to_all | solution.py:57
  162.5 11.2 %all_to_all.105 = f32[16,24,256]{2,1,0:T(8,128)S(1)} all-to-all(f32[16,24,256]{2,1,0:T(8,128)S(1)} %broadcast_in_dim.101), channel_id=1, replica_groups=mesh['seq_0'=4,'seq_1'=4,'seq_2'=2,'batch'=16] {'seq_0','seq_1'}, dimensions={0} | all-to-all | bytes 786432 | tf_op jit(solution)/shard_map/all_to_all | solution.py:21
  173.8 6.9 %all_to_all.106 = f32[2,16,24,256]{3,2,1,0:T(8,128)S(1)} all-to-all(f32[2,16,24,256]{3,2,1,0:T(8,128)S(1)} %broadcast_in_dim.102), channel_id=1, replica_groups=mesh['seq_0'=4,'seq_1'=4,'seq_2'=2,'batch'=16] {'seq_2'}, dimensions={0} | all-to-all | bytes 1572864 | tf_op jit(solution)/shard_map/all_to_all | solution.py:21
  181.2 0.6 fusion.10
  182.3 0.7 convolution_bitcast_fusion.12
  183.5 0.9 convolution_bitcast_fusion.13
  184.4 1.2 convolution_bitcast_fusion.14
  185.7 4.4 %all_to_all.107 = f32[2,16,24,256]{3,2,1,0:T(8,128)S(1)} all-to-all(f32[2,16,24,256]{3,2,1,0:T(8,128)S(1)} %bitcast.239), channel_id=1, replica_groups=mesh['seq_0'=4,'seq_1'=4,'seq_2'=2,'batch'=16] {'seq_2'}, dimensions={0} | all-to-all | bytes 1572864 | tf_op jit(solution)/shard_map/all_to_all | solution.py:49
  190.1 0.8 reduce_sum.135
  190.9 12.8 %all_to_all.108 = f32[16,24,256]{2,1,0:T(8,128)S(1)} all-to-all(f32[16,24,256]{2,1,0:T(8,128)} %reduce_sum.135), channel_id=1, replica_groups=mesh['seq_0'=4,'seq_1'=4,'seq_2'=2,'batch'=16] {'seq_0','seq_1'}, dimensions={0} | all-to-all | bytes 786432 | tf_op jit(solution)/shard_map/all_to_all | solution.py:57
  203.7 11.4 %all_to_all.109 = f32[16,24,256]{2,1,0:T(8,128)S(1)} all-to-all(f32[16,24,256]{2,1,0:T(8,128)S(1)} %broadcast_in_dim.106), channel_id=1, replica_groups=mesh['seq_0'=4,'seq_1'=4,'seq_2'=2,'batch'=16] {'seq_0','seq_1'}, dimensions={0} | all-to-all | bytes 786432 | tf_op jit(solution)/shard_map/all_to_all | solution.py:21
  215.1 6.9 %all_to_all.110 = f32[2,16,24,256]{3,2,1,0:T(8,128)S(1)} all-to-all(f32[2,16,24,256]{3,2,1,0:T(8,128)S(1)} %broadcast_in_dim.107), channel_id=1, replica_groups=mesh['seq_0'=4,'seq_1'=4,'seq_2'=2,'batch'=16] {'seq_2'}, dimensions={0} | all-to-all | bytes 1572864 | tf_op jit(solution)/shard_map/all_to_all | solution.py:21
  222.6 0.6 fusion.8
  223.7 1.2 convolution_bitcast_fusion.11
  225.0 0.9 convolution_bitcast_fusion.10
  225.8 0.7 convolution_bitcast_fusion.9
  226.8 43.5 %all_to_all.111 = f32[16,48,256]{2,1,0:T(8,128)S(1)} all-to-all(f32[16,48,256]{2,1,0:T(8,128)S(1)} %bitcast_subtract_fusion), channel_id=1, replica_groups=mesh['seq_0'=4,'seq_1'=4,'seq_2'=2,'batch'=16] {'batch'}, dimensions={0} | all-to-all | bytes 1572864 | tf_op jit(solution)/shard_map/all_to_all | solution.py:49
  270.4 1.4 broadcast_in_dim.111
  271.7 9.5 %all-to-all-start.18 = ((f32[32,48,256]{2,1,0:T(8,128)}), f32[32,48,256]{2,1,0:T(8,128)S(1)}, u32[]{:S(2)}, u32[]{:S(2)}) async-start(f32[32,48,256]{2,1,0:T(8,128)} %broadcast_in_dim.111), calls=%async_computation.18 | async-start | bytes 3145728 | tf_op jit(solution)/shard_map/all_to_all | solution.py:21
  281.2 2.3 fusion
  283.5 20.3 %all-to-all-done.18 = f32[32,48,256]{2,1,0:T(8,128)S(1)} async-done(((f32[32,48,256]{2,1,0:T(8,128)}), f32[32,48,256]{2,1,0:T(8,128)S(1)}, u32[]{:S(2)}, u32[]{:S(2)}) %all-to-all-start.18) | async-done | bytes 1572896 | tf_op jit(solution)/shard_map/all_to_all | solution.py:21
  303.9 0.7 reduce_sum.141
  (95 shorter events, 6.7 us)
Async XLA Ops:
  0.6 52.1 %copy-start = (bf16[1,512,256]{2,1,0:T(8,128)(2,1)S(1)}, bf16[1,512,256]{2,1,0:T(8,128)(2,1)}, u32[]{:S(2)}) copy-start(bf16[1,512,256]{2,1,0:T(8,128)(2,1)} %param.7) | copy-start | bytes 786436
  0.6 17.6 %copy-start.25 = (f32[1,512]{1,0:T(1,128)S(1)}, f32[1,512]{1,0:T(1,128)}, u32[]{:S(2)}) copy-start(f32[1,512]{1,0:T(1,128)} %param.9) | copy-start | bytes 6148
  0.7 52.5 %copy-start.1 = (bf16[1,512,256]{2,1,0:T(8,128)(2,1)S(1)}, bf16[1,512,256]{2,1,0:T(8,128)(2,1)}, u32[]{:S(2)}) copy-start(bf16[1,512,256]{2,1,0:T(8,128)(2,1)} %param.8) | copy-start | bytes 786436
  2.5 50.2 %all-to-all-start = ((f32[16,48,256]{2,1,0:T(8,128)}), f32[16,48,256]{2,1,0:T(8,128)S(1)}, u32[]{:S(2)}, u32[]{:S(2)}) async-start(f32[16,48,256]{2,1,0:T(8,128)} %broadcast_in_dim.86), calls=%async_computation | async-start | bytes 1572864 | tf_op jit(solution)/shard_map/all_to_all | solution.py:21
  53.1 1.7 copy-start.3
  54.2 1.7 copy-start.12
  54.2 1.7 copy-start.14
  54.2 1.7 copy-start.16
  101.4 0.8 copy-start.5
  102.2 1.7 copy-start.18
  102.3 1.7 copy-start.20
  102.3 1.7 copy-start.22
  141.1 1.0 copy-start.7
  142.1 1.5 copy-start.2
  142.1 1.1 copy-start.24
  142.5 2.4 copy-start.8
  143.2 1.0 copy-start.10
  180.8 1.4 copy-start.6
  180.8 1.4 copy-start.19
  182.3 1.0 copy-start.21
  182.3 1.2 copy-start.23
  222.2 1.4 copy-start.4
  222.2 1.4 copy-start.13
  223.7 1.3 copy-start.15
  223.7 1.3 copy-start.17
  271.7 9.5 %copy-start.9 = (f32[512,256]{1,0:T(8,128)S(1)}, f32[512,256]{1,0:T(8,128)}, u32[]{:S(2)}) copy-start(f32[512,256]{1,0:T(8,128)} %copy-done.8) | copy-start | bytes 1572868
  271.7 9.5 %copy-start.11 = (f32[512,256]{1,0:T(8,128)S(1)}, f32[512,256]{1,0:T(8,128)}, u32[]{:S(2)}) copy-start(f32[512,256]{1,0:T(8,128)} %copy-done.10) | copy-start | bytes 1572868
  271.7 32.1 %all-to-all-start.18 = ((f32[32,48,256]{2,1,0:T(8,128)}), f32[32,48,256]{2,1,0:T(8,128)S(1)}, u32[]{:S(2)}, u32[]{:S(2)}) async-start(f32[32,48,256]{2,1,0:T(8,128)} %broadcast_in_dim.111), calls=%async_computation.18 | async-start | bytes 3145728 | tf_op jit(solution)/shard_map/all_to_all | solution.py:21
where the time goes:
time: 306 us; the launch traced here: 305 us
  blocking collectives  193 us (63%)
  waiting for transfers between devices  54.8 us (18%)
  starting transfers between devices  25.2 us (8%)
  matrix products  21.1 us (7%)
  local copies, waits for them, and re-layouts  5.73 us (2%)
  other arithmetic  3.38 us (1%)
    all_to_all x8, blocking collectives, from_everyone(): return lax.all_to_all(copies, axis, split_axis=0, concat_axis=0, tiled=True)  72.8 us
    all_to_all x5, blocking collectives, sum_at_owner(): lax.all_to_all(in_blocks(value, dim, peers), axis, 0, 0, tiled=True)  66.3 us
    all_to_all x2, waiting for transfers between devices, from_everyone(): return lax.all_to_all(copies, axis, split_axis=0, concat_axis=0, tiled=True)  54.8 us
    all_to_all x4, blocking collectives, summed_rows(): lax.all_to_all(nearer, far, split_axis=0, concat_axis=0, tiled=True)  53.8 us
    all_to_all x2, starting transfers between devices, from_everyone(): return lax.all_to_all(copies, axis, split_axis=0, concat_axis=0, tiled=True)  25.2 us
    dot_general x11, matrix products, swiglu_apply(): jnp.dot(hidden, weights[2].T, precision=high, preferred_element_type=jnp....  10.4 us
  transfers between devices with their start and end apart: 2, of which 2 were waited for; matrix products, arithmetic and copies ran while one was open for 1% of the time, Pallas kernels for 0%

commit v1 on v0

v1 whole, which is shorter than its diff:
```python
import math

import jax
import jax.numpy as jnp
from jax import lax
from jax.experimental import pallas as pl
from jax.experimental.pallas import tpu as pltpu
from jax.sharding import Mesh
from jax.sharding import PartitionSpec as P

MESH = pl.DeviceIdType.MESH
SEQ = ("x", "y", "c")
F32 = jnp.float32
BF16 = jnp.bfloat16
SIDE = 4
CHIPS = SIDE * SIDE
LAYERS = 16
TILE = 8
TOKENS = 512
WIDTH = 256
HALF = 128
GROUPS = 6
ROWS = 256
BOTH = 2 * TOKENS


def far_first():
    hops = lambda step: min(step, SIDE - step)
    steps = [(dx, dy) for dx in range(SIDE) for dy in range(SIDE) if dx or dy]
    return sorted(steps, key=lambda s: -(hops(s[0]) + hops(s[1])))


PEERS = far_first()
NPEERS = len(PEERS)
Z_STEPS = sorted(range(1, LAYERS), key=lambda dz: -min(dz, LAYERS - dz))


def split(value):
    high = value.astype(BF16)
    return high, (value - high.astype(F32)).astype(BF16)


def dot(a, b):
    return jnp.dot(a, b, preferred_element_type=F32)


def kernel(
    q_in, k_in, v_in, rates_in, cot_in, w_in,
    out_ref, grad_ref,
    tok, mine, theirs, tok_b, tok_t, rates_own, rates_other, eta, w_own,
    whole, part, parts, chunk, prev, fin,
    w_ab, w_lo, w_c,
    pre_p, pre_g, pre_u, c1, c2, c3, c4,
    d_hi, d_lo, e_pair, hid, w_ct, out_part, out_other, z_parts, z_sum, tail,
    load_sem, x_send, x_recv, r_send, r_recv, o_send, o_recv,
    rs_send, rs_recv, ag_send, ag_recv, z_send, z_recv, y_send, y_recv, t_send, t_recv, f_send, f_recv,
):
    x, y, c, z = (lax.axis_index(name) for name in ("x", "y", "c", "z"))
    me = x * SIDE + y
    other = (x, y, 1 - c, z)

    loads = [
        pltpu.make_async_copy(src.at[0], tok.at[i], load_sem.at[i])
        for i, src in enumerate((k_in, v_in, q_in, cot_in))
    ]
    loads.append(pltpu.make_async_copy(rates_in, rates_own, load_sem.at[4]))
    for load in loads:
        load.start()

    def peer(step):
        px = lax.rem(x + step[0], SIDE)
        py = lax.rem(y + step[1], SIDE)
        return (px, py, c, z), px * SIDE + py

    def z_peer(dz):
        return (x, y, c, lax.rem(z + dz, LAYERS))

    barrier = pltpu.get_barrier_semaphore()
    for dz in Z_STEPS:
        pl.semaphore_signal(barrier, inc=1, device_id=z_peer(dz), device_id_type=MESH)
    for step in PEERS:
        pl.semaphore_signal(barrier, inc=1, device_id=peer(step)[0], device_id_type=MESH)
    pl.semaphore_signal(barrier, inc=1, device_id=other, device_id_type=MESH)

    for half in range(2):
        @pl.when(c == half)
        def _():
            w_own[...] = w_in[:, half * HALF : (half + 1) * HALF].reshape(GROUPS, TILE, HALF)

    for load in loads:
        load.wait()
    for i in range(4):
        mine[i] = tok[i].astype(F32)
    divisor = math.sqrt(lax.axis_size(SEQ) * TOKENS)
    eta[0:TOKENS] = -jnp.broadcast_to(rates_own[...] / divisor, (HALF, TOKENS)).T

    pl.semaphore_wait(barrier, LAYERS - 1 + NPEERS + 1)

    sub = lax.rem(me + GROUPS * LAYERS - GROUPS * z, CHIPS)
    group = GROUPS * z + sub
    at = lax.div(group, CHIPS)

    def z_copy(dz):
        return pltpu.make_async_remote_copy(
            w_own.at[sub], chunk.at[at], z_send.at[dz - 1], z_recv.at[at],
            device_id=z_peer(dz), device_id_type=MESH,
        )

    @pl.when(sub < GROUPS)
    def _():
        for dz in Z_STEPS:
            z_copy(dz).start()
        chunk[pl.ds(at, 1)] = w_own[pl.ds(sub, 1)]

    swaps = [
        pltpu.make_async_remote_copy(
            mine.at[i], theirs.at[i], x_send.at[i], x_recv.at[i], device_id=other, device_id_type=MESH
        )
        for i in range(4)
    ]
    swaps.append(
        pltpu.make_async_remote_copy(
            rates_own, rates_other, r_send, r_recv, device_id=other, device_id_type=MESH
        )
    )
    for swap in swaps:
        swap.start()

    for i in range(4):
        tok_b[i, 0:TOKENS] = tok[i]
        tok_t[i, :, 0:TOKENS] = mine[i].T.astype(BF16)
    for swap in swaps:
        swap.wait()
    eta[TOKENS:BOTH] = -jnp.broadcast_to(rates_other[...] / divisor, (HALF, TOKENS)).T
    for i in range(4):
        tok_b[i, TOKENS:BOTH] = theirs[i].astype(BF16)
        tok_t[i, :, TOKENS:BOTH] = theirs[i].T.astype(BF16)

    for j in range(GROUPS):
        owner = lax.div(CHIPS * j + me, GROUPS)

        @pl.when(owner != z)
        def _():
            pltpu.make_async_remote_copy(
                w_own.at[0], chunk.at[j], z_send.at[0], z_recv.at[j], device_id=other, device_id_type=MESH
            ).wait_recv()

    @pl.when(sub < GROUPS)
    def _():
        for dz in Z_STEPS:
            z_copy(dz).wait_send()

    def gather(stage):
        copies = [
            pltpu.make_async_remote_copy(
                chunk, whole.at[stage, :, me], ag_send.at[k], ag_recv.at[k],
                device_id=peer(step)[0], device_id_type=MESH,
            )
            for k, step in enumerate(PEERS)
        ]
        for copy in copies:
            copy.start()
        whole[stage, :, pl.ds(me, 1)] = chunk[...].reshape(GROUPS, 1, TILE, HALF)
        return copies

    def scatter():
        copies = []
        for k, step in enumerate(PEERS):
            device, chip = peer(step)
            copies.append(
                pltpu.make_async_remote_copy(
                    part.at[:, chip], parts.at[k], rs_send.at[k], rs_recv.at[k],
                    device_id=device, device_id_type=MESH,
                )
            )
        for copy in copies:
            copy.start()
        return copies

    def reduced(copies):
        for copy in copies:
            copy.wait()
        total = part[:, pl.ds(me, 1)].reshape(GROUPS, TILE, HALF)
        for k in range(NPEERS):
            total = total + parts[k]
        return total

    def weights(stage):
        for i in range(2):
            high, low = split(whole[stage, 2 * i : 2 * i + 2].reshape(WIDTH, HALF))
            w_ab[:, i * HALF : (i + 1) * HALF] = high
            w_lo[:, i * HALF : (i + 1) * HALF] = low
        high, low = split(whole[stage, 4:6].reshape(WIDTH, HALF))
        w_c[:, 0:HALF] = high
        w_c[:, HALF:] = low

    def projected(first, second, rows):
        pg = dot(tok_b[first, rows], w_ab[...]) + dot(tok_b[first, rows], w_lo[...])
        uu = dot(tok_b[second, rows], w_c[...])
        return pg[:, :HALF], pg[:, HALF:], uu[:, :HALF] + uu[:, HALF:]

    def keep(rows, dp, dg, e):
        for i, value in enumerate((dp, dg)):
            high, low = split(value)
            d_hi[rows, i * HALF : (i + 1) * HALF] = high
            d_lo[rows, i * HALF : (i + 1) * HALF] = low
        high, low = split(e)
        e_pair[rows, 0:HALF] = high
        e_pair[rows, HALF:] = low

    def contract(first, second):
        ab = dot(tok_t[first], d_hi[...]) + dot(tok_t[first], d_lo[...])
        cc = dot(tok_t[second], e_pair[...])
        part[0:2] = ab[:, :HALF].reshape(2, CHIPS, TILE, HALF)
        part[2:4] = ab[:, HALF:].reshape(2, CHIPS, TILE, HALF)
        part[4:6] = (cc[:, :HALF] + cc[:, HALF:]).reshape(2, CHIPS, TILE, HALF)

    def token_loop(body):
        def step(i, carry):
            body(pl.ds(pl.multiple_of(i * ROWS, ROWS), ROWS))
            return carry

        lax.fori_loop(0, BOTH // ROWS, step, 0)

    def sigmoid(g):
        return 1.0 / (1.0 + jnp.exp(-g))

    def inner(stage):
        weights(stage)

        def body(rows):
            p, g, u = projected(0, 1, rows)
            s = sigmoid(g)
            act = g * s
            slope = s + act * (1.0 - s)
            rate = eta[rows]
            f1 = rate * act
            f3 = rate * p * slope
            pre_p[rows] = p
            pre_g[rows] = g
            pre_u[rows] = u
            c1[stage, rows] = f1
            c3[stage, rows] = f3
            keep(rows, f1 * u, f3 * u, f1 * p)

        token_loop(body)
        contract(0, 1)

    def inner_second(stage):
        def body(rows):
            p, g, u = pre_p[rows], pre_g[rows], pre_u[rows]
            s = sigmoid(g)
            slope = s + g * s * (1.0 - s)
            bend = s * (1.0 - s) * (2.0 + g * (1.0 - 2.0 * s))
            w = eta[rows] * u
            c2[stage, rows] = w * slope
            c4[stage, rows] = w * p * bend

        token_loop(body)

    def hessian(stage, direction):
        weights(direction)

        def body(rows):
            p, g, u = projected(0, 1, rows)
            f1, f2, f3, f4 = c1[stage, rows], c2[stage, rows], c3[stage, rows], c4[stage, rows]
            keep(rows, f1 * u + f2 * g, f3 * u + f2 * p + f4 * g, f3 * g + f1 * p)

        token_loop(body)
        contract(0, 1)

    prev[...] = chunk[...]
    gathers = gather(0)
    for copy in gathers:
        copy.wait()
    for stage in range(2):
        inner(stage)
        copies = scatter()
        inner_second(stage)
        chunk[...] = prev[...] - reduced(copies)
        prev[...] = chunk[...]
        gathers = gather(stage + 1)
        for copy in gathers:
            copy.wait()

    weights(2)
    w_ct[0:HALF] = w_c[:, 0:HALF].astype(F32).T.astype(BF16)
    w_ct[HALF:] = w_c[:, HALF:].astype(F32).T.astype(BF16)

    def outer(rows):
        p, g, u = projected(2, 3, rows)
        s = sigmoid(g)
        act = g * s
        slope = s + act * (1.0 - s)
        h = act * p
        keep(rows, u * act, u * p * slope, h)

    token_loop(outer)
    contract(2, 3)
    copies = scatter()

    def partial_out(rows):
        high = e_pair[rows, 0:HALF]
        low = e_pair[rows, HALF:]
        return dot(high, w_ct[0:HALF]) + (dot(high, w_ct[HALF:]) + dot(low, w_ct[0:HALF]))

    out_part[...] = partial_out(pl.ds(TOKENS, TOKENS))
    swap = pltpu.make_async_remote_copy(
        out_part, out_other, o_send, o_recv, device_id=other, device_id_type=MESH
    )
    swap.start()
    hid[...] = partial_out(pl.ds(0, TOKENS))
    chunk[...] = reduced(copies)
    prev[...] = chunk[...]
    gathers = gather(3)
    swap.wait()
    out_ref[0] = (hid[...] + out_other[...]).astype(BF16)
    for copy in gathers:
        copy.wait()

    hessian(1, 3)
    copies = scatter()
    chunk[...] = prev[...] - reduced(copies)
    prev[...] = chunk[...]
    gathers = gather(4)
    for copy in gathers:
        copy.wait()

    hessian(0, 4)
    copies = scatter()
    fin[...] = prev[...] - reduced(copies)

    def to_owner(j):
        target_group = CHIPS * j + me
        target = lax.div(target_group, GROUPS)
        slot = lax.rem(target + LAYERS - z, LAYERS)
        return target, pltpu.make_async_remote_copy(
            fin.at[j], z_parts.at[slot], y_send.at[j], y_recv.at[slot],
            device_id=(x, y, c, target), device_id_type=MESH,
        )

    for j in range(GROUPS):
        target, copy = to_owner(j)

        @pl.when(target != z)
        def _():
            copy.start()

    @pl.when(sub < GROUPS)
    def _():
        total = fin[pl.ds(at, 1)].reshape(TILE, HALF)
        for slot in range(1, LAYERS):
            pltpu.make_async_remote_copy(
                fin.at[0], z_parts.at[slot], y_send.at[0], y_recv.at[slot],
                device_id=other, device_id_type=MESH,
            ).wait_recv()
        for slot in range(1, LAYERS):
            total = total + z_parts[slot]
        z_sum[...] = total
        tail[pl.ds(c, 1), pl.ds(sub, 1)] = total.reshape(1, 1, TILE, HALF)
        for k, step in enumerate(PEERS):
            pltpu.make_async_remote_copy(
                z_sum, tail.at[c, sub], t_send.at[k], t_recv.at[sub],
                device_id=peer(step)[0], device_id_type=MESH,
            ).start()

    for j in range(GROUPS):
        target, copy = to_owner(j)

        @pl.when(target != z)
        def _():
            copy.wait_send()

    for s in range(GROUPS):
        source = lax.rem(GROUPS * z + s, CHIPS)

        @pl.when(source != me)
        def _():
            pltpu.make_async_remote_copy(
                z_sum, tail.at[c, s], t_send.at[0], t_recv.at[s], device_id=other, device_id_type=MESH
            ).wait_recv()

    swap = pltpu.make_async_remote_copy(
        tail.at[c], tail.at[c], f_send, f_recv, device_id=other, device_id_type=MESH
    )
    swap.start()

    @pl.when(sub < GROUPS)
    def _():
        for k, step in enumerate(PEERS):
            pltpu.make_async_remote_copy(
                z_sum, tail.at[c, sub], t_send.at[k], t_recv.at[sub],
                device_id=peer(step)[0], device_id_type=MESH,
            ).wait_send()

    swap.wait()
    for half in range(2):
        grad_ref[:, half * HALF : (half + 1) * HALF] = tail[half].reshape(GROUPS * TILE, HALF)


def body(queries, key_rows, value_rows, step_rates, cotangent, fast_init):
    vmem = lambda *shape: pltpu.VMEM(shape, F32)
    half = lambda *shape: pltpu.VMEM(shape, BF16)
    dma = lambda *shape: pltpu.SemaphoreType.DMA(shape)
    any_spec = pl.BlockSpec(memory_space=pl.ANY)
    vmem_spec = pl.BlockSpec(memory_space=pltpu.VMEM)
    return pl.pallas_call(
        kernel,
        out_shape=(
            jax.ShapeDtypeStruct(queries.shape, BF16),
            jax.ShapeDtypeStruct(fast_init.shape, F32),
        ),
        in_specs=[any_spec] * 5 + [vmem_spec],
        out_specs=(vmem_spec, vmem_spec),
        scratch_shapes=[
            half(4, TOKENS, WIDTH),
            vmem(4, TOKENS, WIDTH),
            vmem(4, TOKENS, WIDTH),
            half(4, BOTH, WIDTH),
            half(4, WIDTH, BOTH),
            vmem(1, TOKENS),
            vmem(1, TOKENS),
            vmem(BOTH, HALF),
            vmem(GROUPS, TILE, HALF),
            vmem(5, GROUPS, CHIPS, TILE, HALF),
            vmem(GROUPS, CHIPS, TILE, HALF),
            vmem(NPEERS, GROUPS, TILE, HALF),
            vmem(GROUPS, TILE, HALF),
            vmem(GROUPS, TILE, HALF),
            vmem(GROUPS, TILE, HALF),
            half(WIDTH, WIDTH),
            half(WIDTH, WIDTH),
            half(WIDTH, WIDTH),
            vmem(BOTH, HALF),
            vmem(BOTH, HALF),
            vmem(BOTH, HALF),
            vmem(2, BOTH, HALF),
            vmem(2, BOTH, HALF),
            vmem(2, BOTH, HALF),
            vmem(2, BOTH, HALF),
            half(BOTH, WIDTH),
            half(BOTH, WIDTH),
            half(BOTH, WIDTH),
            vmem(TOKENS, WIDTH),
            half(WIDTH, WIDTH),
            vmem(TOKENS, WIDTH),
            vmem(TOKENS, WIDTH),
            vmem(LAYERS, TILE, HALF),
            vmem(TILE, HALF),
            vmem(2, GROUPS, TILE, HALF),
            dma(5),
            dma(4), dma(4),
            pltpu.SemaphoreType.DMA, pltpu.SemaphoreType.DMA,
            pltpu.SemaphoreType.DMA, pltpu.SemaphoreType.DMA,
            dma(NPEERS), dma(NPEERS),
            dma(NPEERS), dma(NPEERS),
            dma(LAYERS), dma(GROUPS),
            dma(GROUPS), dma(LAYERS),
            dma(NPEERS), dma(GROUPS),
            pltpu.SemaphoreType.DMA, pltpu.SemaphoreType.DMA,
        ],
        compiler_params=pltpu.CompilerParams(
            collective_id=0, has_side_effects=True, vmem_limit_bytes=56 * 2**20
        ),
    )(queries, key_rows, value_rows, step_rates, cotangent, fast_init)


def solution(mesh):
    torus = Mesh(
        mesh.devices.reshape(SIDE, SIDE, 2, mesh.shape["batch"]), ("x", "y", "c", "z")
    )
    return jax.shard_map(
        body,
        mesh=torus,
        in_specs=(
            P("z", SEQ, None),
            P("z", SEQ, None),
            P("z", SEQ, None),
            P("z", SEQ),
            P("z", SEQ, None),
            P("z", None),
        ),
        out_specs=(P("z", SEQ, None), P("z", None)),
        check_vma=False,
    )
```

time: 306 us -> 115 us (0.38)
  blocking collectives: 193 us -> 0 us
  Pallas kernels: 0 us -> 112 us
  waiting for transfers between devices: 54.8 us -> 0 us
  starting transfers between devices: 25.2 us -> 0 us
  matrix products: 21.1 us -> 0 us
  local copies, waits for them, and re-layouts: 5.73 us -> 2.31 us
  other arithmetic: 3.38 us -> 0 us
    all_to_all x17 -> x0, blocking collectives: 193 us -> none  [the longest x8 72.8 us: from_everyone(): return lax.all_to_all(copies, axis, split_axis=0, concat_axis=0, tiled=True)]
    pallas_call x0 -> x1, Pallas kernels: none -> 112 us  [body(): pl.pallas_call(kernel, out_shape=(jax.ShapeDtypeStruct(queries.shape, BF1...]
    all_to_all x2 -> x0, waiting for transfers between devices: 54.8 us -> none  [from_everyone(): return lax.all_to_all(copies, axis, split_axis=0, concat_axis=0, tiled=True)]
    all_to_all x2 -> x0, starting transfers between devices: 25.2 us -> none  [from_everyone(): return lax.all_to_all(copies, axis, split_axis=0, concat_axis=0, tiled=True)]
    dot_general x31 -> x0, matrix products: 21.1 us -> none  [the longest x11 10.4 us: swiglu_apply(): jnp.dot(hidden, weights[2].T, precision=high, preferred_element_type=jnp....]
    broadcast_in_dim x10 -> x0, local copies, waits for them, and re-layouts: 3.49 us -> none  [from_everyone(): copies = jnp.broadcast_to(value, (lax.axis_size(axis), *value.shape))]
  transfers between devices with their start and end apart: 2 -> 0, of which waited for: 2 -> 0; matrix products, arithmetic and copies ran while one was open for 1% -> 0% of each run, Pallas kernels for 0% -> 0%
where the time goes in v1:
time: 115 us
  Pallas kernels  112 us (97%)
  local copies, waits for them, and re-layouts  2.31 us (2%)
    pallas_call x1, Pallas kernels, body(): pl.pallas_call(kernel, out_shape=(jax.ShapeDtypeStruct(queries.shape, BF1...  112 us
    unnamed x4, local copies, waits for them, and re-layouts  2.31 us

profile of v1, /device:TPU:1, one launch (start us, length us, event | category | flops | bytes accessed | tf_op | source)
XLA Modules:
  0.0 114.9 jit_solution(11244435692135870932)
XLA Ops:
  0.6 112.0 %shard_map.77 = (bf16[1,512,256]{2,1,0:T(8,128)(2,1)}, f32[48,256]{1,0:T(8,128)}) custom-call(bf16[1,512,256]{2,1,0:T(8,128)(2,1)} %q_in.1, bf16[1,512,256]{2,1,0:T(8,128)(2,1)} %k_in.1, bf16[1,512,256]{2,1,0:T(8,128)(2,1)} %v_in.1, f32[1,512]{1,0:T(1,128)} %rates_in.1, bf16[1,512,256]{2,1,0:T(8,128)(2,1)} %cot_in.1, f32[48,256]{1,0:T(8,128)} %w_in.1), custom_call_target="tpu_custom_call" | custom-call | tf_op jit(solution)/shard_map/pallas_call | solution.py:407
  112.6 0.0 copy-start
  112.6 1.7 %copy.10 = bf16[1,512,256]{2,1,0:T(8,128)(2,1)} copy(bf16[1,512,256]{2,1,0:T(8,128)(2,1)} %get-tuple-element.4) | data formatting | bytes 524288
  114.3 0.0 copy-done
  114.3 0.6 copy.11
Async XLA Ops:
  112.6 1.7 %copy-start = (f32[48,256]{1,0:T(8,128)S(1)}, f32[48,256]{1,0:T(8,128)}, u32[]{:S(2)}) copy-start(f32[48,256]{1,0:T(8,128)} %get-tuple-element.5) | copy-start | bytes 147460

commit v2 on v1

v2 whole, which is shorter than its diff:
```python
import math

import jax
import jax.numpy as jnp
from jax import lax
from jax.experimental import pallas as pl
from jax.experimental.pallas import tpu as pltpu
from jax.sharding import Mesh
from jax.sharding import PartitionSpec as P

MESH = pl.DeviceIdType.MESH
SEQ = ("x", "y", "c")
F32 = jnp.float32
BF16 = jnp.bfloat16
SIDE = 4
CHIPS = SIDE * SIDE
LAYERS = 16
TILE = 8
TOKENS = 512
WIDTH = 256
HALF = 128
GROUPS = 6
COLS = 256
BOTH = 2 * TOKENS
PIPES = 2
UNITS = HALF // PIPES
HEIGHT = 3 * UNITS
TILES = 2 * HEIGHT // TILE
OWNED = TILES // CHIPS
NEAR = 4


def far_first():
    hops = lambda step: min(step, SIDE - step)
    steps = [(dx, dy) for dx in range(SIDE) for dy in range(SIDE) if dx or dy]
    return sorted(steps, key=lambda s: -(hops(s[0]) + hops(s[1])))


PEERS = far_first()
NPEERS = len(PEERS)
Z_STEPS = [d for dz in range(NEAR, 0, -1) for d in (dz, LAYERS - dz)]


def split(value):
    high = value.astype(BF16)
    return high, (value - high.astype(F32)).astype(BF16)


def dot(a, b):
    return jnp.dot(a, b, preferred_element_type=F32)


def kernel(
    q_in, k_in, v_in, rates_in, cot_in, w_in,
    out_ref, grad_ref,
    tok, mine, theirs, tok_b, tok_t, rates_own, rates_other, eta, w_own,
    natural, n_part, n_parts, n_chunk, n_adj,
    whole, part, parts, chunk,
    lhs_ab, lhs_c,
    pre_p, pre_g, pre_u, c1, c2, c3, c4,
    d_pair, e_pair, out_own, out_part, out_other, z_parts, z_sum, tail,
    load_sem, x_send, x_recv, r_send, r_recv, o_send, o_recv,
    n_send, n_recv, rs_send, rs_recv, ag_send, ag_recv,
    z_send, z_recv, zz_send, y_send, y_recv, t_send, t_recv,
):
    x, y, c, z = (lax.axis_index(name) for name in ("x", "y", "c", "z"))
    me = x * SIDE + y
    other = (x, y, 1 - c, z)

    loads = [
        pltpu.make_async_copy(src.at[0], tok.at[i], load_sem.at[i])
        for i, src in enumerate((k_in, v_in, q_in, cot_in))
    ]
    loads.append(pltpu.make_async_copy(rates_in, rates_own, load_sem.at[4]))
    for load in loads:
        load.start()

    def peer(step):
        px = lax.rem(x + step[0], SIDE)
        py = lax.rem(y + step[1], SIDE)
        return (px, py, c, z), px * SIDE + py

    def z_peer(dz):
        return (x, y, c, lax.rem(z + dz, LAYERS))

    peers = [peer(step) for step in PEERS]
    everyone = [(d[0], d[1], core, z) for d, _ in peers for core in (c, 1 - c)] + [other]

    barrier = pltpu.get_barrier_semaphore()
    greeted = [z_peer(dz) for dz in Z_STEPS] + everyone
    for device in greeted:
        pl.semaphore_signal(barrier, inc=1, device_id=device, device_id_type=MESH)

    for half in range(2):
        @pl.when(c == half)
        def _():
            w_own[...] = w_in[:, half * HALF : (half + 1) * HALF].reshape(GROUPS, TILE, HALF)

    divisor = math.sqrt(lax.axis_size(SEQ) * TOKENS)
    for load in loads:
        load.wait()
    for i in range(4):
        mine[i] = tok[i].astype(F32)
    eta[:, 0:TOKENS] = jnp.broadcast_to(-(rates_own[...] / divisor), (TILE, TOKENS))

    pl.semaphore_wait(barrier, len(greeted))

    sub = lax.rem(me + GROUPS * LAYERS - GROUPS * z, CHIPS)
    group = GROUPS * z + sub
    at = lax.div(group, CHIPS)
    owner = sub < GROUPS

    def z_copy(i):
        return pltpu.make_async_remote_copy(
            w_own.at[sub], n_chunk.at[at], z_send.at[i], z_recv.at[at],
            device_id=z_peer(Z_STEPS[i]), device_id_type=MESH,
        )

    @pl.when(owner)
    def _():
        for i in range(len(Z_STEPS)):
            z_copy(i).start()
        n_chunk[pl.ds(at, 1)] = w_own[pl.ds(sub, 1)]

    swaps = [
        pltpu.make_async_remote_copy(
            mine.at[i], theirs.at[i], x_send.at[i], x_recv.at[i], device_id=other, device_id_type=MESH
        )
        for i in range(4)
    ]
    swaps.append(
        pltpu.make_async_remote_copy(
            rates_own, rates_other, r_send, r_recv, device_id=other, device_id_type=MESH
        )
    )
    for swap in swaps:
        swap.start()

    def own_tokens(i):
        tok_b[i, 0:TOKENS] = tok[i]
        tok_t[i, :, 0:TOKENS] = mine[i].T.astype(BF16)

    def other_tokens(i):
        swaps[i].wait()
        tok_b[i, TOKENS:BOTH] = theirs[i].astype(BF16)
        tok_t[i, :, TOKENS:BOTH] = theirs[i].T.astype(BF16)

    for i in range(2):
        own_tokens(i)

    def z_pass(j, steps):
        dz = NEAR if steps > 0 else LAYERS - NEAR
        return pltpu.make_async_remote_copy(
            n_chunk.at[j], n_chunk.at[j], zz_send.at[j], z_recv.at[j],
            device_id=z_peer(dz), device_id_type=MESH,
        )

    def z_away(j):
        return lax.rem(z + LAYERS - lax.div(CHIPS * j + me, GROUPS), LAYERS)

    def z_landed(j):
        pltpu.make_async_remote_copy(
            w_own.at[0], n_chunk.at[j], z_send.at[0], z_recv.at[j], device_id=other, device_id_type=MESH
        ).wait_recv()

    def up(j):
        return (z_away(j) >= 1) & (z_away(j) <= NEAR)

    def down(j):
        return z_away(j) >= LAYERS - NEAR + 1

    for j in range(GROUPS):
        @pl.when(up(j))
        def _():
            z_landed(j)
            z_pass(j, 1).start()

        @pl.when(down(j))
        def _():
            z_landed(j)
            z_pass(j, -1).start()

        @pl.when(z_away(j) == LAYERS - NEAR)
        def _():
            z_landed(j)

    for i in range(2):
        other_tokens(i)
    swaps[4].wait()
    eta[:, TOKENS:BOTH] = jnp.broadcast_to(-(rates_other[...] / divisor), (TILE, TOKENS))

    for j in range(GROUPS):
        @pl.when((z_away(j) > NEAR) & (z_away(j) < LAYERS - NEAR))
        def _():
            z_landed(j)

    firsts = [
        pltpu.make_async_remote_copy(
            n_chunk, natural.at[:, me], n_send.at[k], n_recv.at[k], device_id=device, device_id_type=MESH
        )
        for k, (device, _) in enumerate(peers)
    ]
    for copy in firsts:
        copy.start()
    natural[:, pl.ds(me, 1)] = n_chunk[...].reshape(GROUPS, 1, TILE, HALF)

    for i in (2, 3):
        own_tokens(i)
        other_tokens(i)

    @pl.when(owner)
    def _():
        for i in range(len(Z_STEPS)):
            z_copy(i).wait_send()

    for j in range(GROUPS):
        @pl.when(up(j))
        def _():
            z_pass(j, 1).wait_send()

        @pl.when(down(j))
        def _():
            z_pass(j, -1).wait_send()

    def gathering(stage, pipe):
        return [
            pltpu.make_async_remote_copy(
                chunk.at[pipe], whole.at[stage, pipe, :, me], ag_send.at[pipe, k], ag_recv.at[pipe, k],
                device_id=device, device_id_type=MESH,
            )
            for k, (device, _) in enumerate(peers)
        ]

    def scattering(pipe):
        return [
            pltpu.make_async_remote_copy(
                part.at[pipe, :, chip], parts.at[pipe, k], rs_send.at[pipe, k], rs_recv.at[pipe, k],
                device_id=device, device_id_type=MESH,
            )
            for k, (device, chip) in enumerate(peers)
        ]

    def reduced(pipe):
        for copy in scattering(pipe):
            copy.wait()
        total = part[pipe, :, pl.ds(me, 1)].reshape(OWNED, TILE, HALF)
        for k in range(NPEERS):
            total = total + parts[pipe, k]
        return total

    def gather(stage, pipe, value):
        chunk[pipe] = value
        for copy in gathering(stage, pipe):
            copy.start()
        whole[stage, pipe, :, pl.ds(me, 1)] = value.reshape(OWNED, 1, TILE, HALF)

    def gathered(stage, pipe):
        for copy in gathering(stage, pipe):
            copy.wait()

    def from_tiles(tiles):
        flat = tiles.reshape(TILES, TILE, HALF)
        left = flat[: TILES // 2].reshape(HEIGHT, HALF)
        right = flat[TILES // 2 :].reshape(HEIGHT, HALF)
        return jnp.concatenate([left, right], axis=1)

    def to_tiles(value):
        left = value[:, :HALF].reshape(TILES // 2, TILE, HALF)
        right = value[:, HALF:].reshape(TILES // 2, TILE, HALF)
        return jnp.concatenate([left, right], axis=0).reshape(OWNED, CHIPS, TILE, HALF)

    def weights(stage, pipe):
        high, low = split(from_tiles(whole[stage, pipe]))
        lhs_ab[0 : 2 * UNITS] = high[: 2 * UNITS]
        lhs_ab[2 * UNITS :] = low[: 2 * UNITS]
        lhs_c[0:UNITS] = high[2 * UNITS :]
        lhs_c[UNITS:] = low[2 * UNITS :]

    def projected(first, second, cols):
        pg = dot(lhs_ab[...], tok_t[first, :, cols])
        pg = pg[: 2 * UNITS] + pg[2 * UNITS :]
        uu = dot(lhs_c[...], tok_t[second, :, cols])
        return pg[:UNITS], pg[UNITS:], uu[:UNITS] + uu[UNITS:]

    def keep(cols, dp, dg, e, pipe):
        for i, value in enumerate((dp, dg)):
            high, low = split(value)
            d_pair[i * UNITS : (i + 1) * UNITS, cols] = high
            d_pair[(2 + i) * UNITS : (3 + i) * UNITS, cols] = low
        high, low = split(e)
        e_pair[pipe, 0:UNITS, cols] = high
        e_pair[pipe, UNITS:, cols] = low

    def contract(first, second, pipe):
        ab = dot(d_pair[...], tok_b[first])
        cc = dot(e_pair[pipe], tok_b[second])
        return jnp.concatenate(
            [ab[: 2 * UNITS] + ab[2 * UNITS :], cc[:UNITS] + cc[UNITS:]], axis=0
        )

    def scatter(pipe, value):
        part[pipe] = to_tiles(value)
        for copy in scattering(pipe):
            copy.start()

    def token_loop(body):
        for i in range(BOTH // COLS):
            body(slice(i * COLS, (i + 1) * COLS))

    def sigmoid(g):
        return 1.0 / (1.0 + jnp.exp(-g))

    def rates(cols):
        return jnp.concatenate([eta[:, cols]] * (UNITS // TILE), axis=0)

    def inner(stage, pipe):
        weights(stage, pipe)

        def body(cols):
            p, g, u = projected(0, 1, cols)
            s = sigmoid(g)
            act = g * s
            slope = s + act * (1.0 - s)
            rate = rates(cols)
            f1 = rate * act
            f3 = rate * p * slope
            pre_p[pipe, :, cols] = p
            pre_g[pipe, :, cols] = g
            pre_u[pipe, :, cols] = u
            c1[stage, pipe, :, cols] = f1
            c3[stage, pipe, :, cols] = f3
            keep(cols, f1 * u, f3 * u, f1 * p, pipe)

        token_loop(body)
        return contract(0, 1, pipe)

    def inner_second(stage, pipe):
        def body(cols):
            p, g, u = pre_p[pipe, :, cols], pre_g[pipe, :, cols], pre_u[pipe, :, cols]
            s = sigmoid(g)
            slope = s + g * s * (1.0 - s)
            bend = s * (1.0 - s) * (2.0 + g * (1.0 - 2.0 * s))
            w = rates(cols) * u
            c2[stage, pipe, :, cols] = w * slope
            c4[stage, pipe, :, cols] = w * p * bend

        token_loop(body)

    def outer(pipe):
        weights(2, pipe)

        def body(cols):
            p, g, u = projected(2, 3, cols)
            s = sigmoid(g)
            act = g * s
            slope = s + act * (1.0 - s)
            keep(cols, u * act, u * p * slope, act * p, pipe)

        token_loop(body)
        return contract(2, 3, pipe)

    def hessian(stage, direction, pipe):
        weights(direction, pipe)

        def body(cols):
            p, g, u = projected(0, 1, cols)
            f1, f2 = c1[stage, pipe, :, cols], c2[stage, pipe, :, cols]
            f3, f4 = c3[stage, pipe, :, cols], c4[stage, pipe, :, cols]
            keep(cols, f1 * u + f2 * g, f3 * u + f2 * p + f4 * g, f3 * g + f1 * p, pipe)

        token_loop(body)
        return contract(0, 1, pipe)

    for copy in firsts:
        copy.wait()
    flipped = [
        natural[2 * i : 2 * i + 2].reshape(WIDTH, HALF).T for i in range(3)
    ]
    for pipe in range(PIPES):
        rows = slice(pipe * UNITS, (pipe + 1) * UNITS)
        whole[0, pipe] = to_tiles(jnp.concatenate([matrix[rows] for matrix in flipped], axis=0))

    def mine_of(stage, pipe):
        return whole[stage, pipe, :, pl.ds(me, 1)].reshape(OWNED, TILE, HALF)

    for pipe in range(PIPES):
        scatter(pipe, inner(0, pipe))
    for pipe in range(PIPES):
        inner_second(0, pipe)
    for pipe in range(PIPES):
        gather(1, pipe, mine_of(0, pipe) - reduced(pipe))
    for pipe in range(PIPES):
        gathered(1, pipe)
        scatter(pipe, inner(1, pipe))
    for pipe in range(PIPES):
        inner_second(1, pipe)
    for pipe in range(PIPES):
        gather(2, pipe, mine_of(1, pipe) - reduced(pipe))

    for pipe in range(PIPES):
        gathered(2, pipe)
        scatter(pipe, outer(pipe))

    def partial_out(cols):
        total = None
        for pipe in range(PIPES):
            ct_high, ct_low = split(from_tiles(whole[2, pipe])[2 * UNITS :])
            high = e_pair[pipe, 0:UNITS, cols].astype(F32).T.astype(BF16)
            low = e_pair[pipe, UNITS:, cols].astype(F32).T.astype(BF16)
            term = dot(high, ct_high) + (dot(high, ct_low) + dot(low, ct_high))
            total = term if total is None else total + term
        return total

    out_part[...] = partial_out(slice(TOKENS, BOTH))
    swap = pltpu.make_async_remote_copy(
        out_part, out_other, o_send, o_recv, device_id=other, device_id_type=MESH
    )
    swap.start()
    out_own[...] = partial_out(slice(0, TOKENS))
    for pipe in range(PIPES):
        gather(3, pipe, reduced(pipe))
    swap.wait()
    out_ref[0] = (out_own[...] + out_other[...]).astype(BF16)

    for pipe in range(PIPES):
        gathered(3, pipe)
        scatter(pipe, hessian(1, 3, pipe))
    for pipe in range(PIPES):
        gather(4, pipe, mine_of(3, pipe) - reduced(pipe))

    def upright(values):
        for i in range(3):
            rows = slice(i * UNITS, (i + 1) * UNITS)
            matrix = jnp.concatenate([value[rows] for value in values], axis=0)
            yield matrix.T.reshape(2, CHIPS, TILE, HALF)

    terms = []
    for pipe in range(PIPES):
        gathered(4, pipe)
        terms.append(hessian(0, 4, pipe))
    for i, value in enumerate(upright(terms)):
        n_part[2 * i : 2 * i + 2] = value
    lasts = [
        pltpu.make_async_remote_copy(
            n_part.at[:, chip], n_parts.at[k], n_send.at[k], n_recv.at[k],
            device_id=device, device_id_type=MESH,
        )
        for k, (device, chip) in enumerate(peers)
    ]
    for copy in lasts:
        copy.start()
    for i, value in enumerate(upright([from_tiles(whole[4, pipe]) for pipe in range(PIPES)])):
        n_adj[2 * i : 2 * i + 2] = value
    total = (n_adj[:, pl.ds(me, 1)] - n_part[:, pl.ds(me, 1)]).reshape(GROUPS, TILE, HALF)
    for copy in lasts:
        copy.wait()
    for k in range(NPEERS):
        total = total - n_parts[k]
    n_chunk[...] = total

    def to_owner(j):
        target = lax.div(CHIPS * j + me, GROUPS)
        slot = lax.rem(target + LAYERS - z, LAYERS)
        return target, pltpu.make_async_remote_copy(
            n_chunk.at[j], z_parts.at[slot], y_send.at[j], y_recv.at[slot],
            device_id=(x, y, c, target), device_id_type=MESH,
        )

    for j in range(GROUPS):
        target, copy = to_owner(j)

        @pl.when(target != z)
        def _():
            copy.start()

    def spread():
        return [
            pltpu.make_async_remote_copy(
                z_sum, tail.at[c, sub], t_send.at[k], t_recv.at[c, sub],
                device_id=device, device_id_type=MESH,
            )
            for k, device in enumerate(everyone)
        ]

    @pl.when(owner)
    def _():
        for slot in range(1, LAYERS):
            pltpu.make_async_remote_copy(
                n_chunk.at[0], z_parts.at[slot], y_send.at[0], y_recv.at[slot],
                device_id=other, device_id_type=MESH,
            ).wait_recv()
        total = n_chunk[pl.ds(at, 1)].reshape(TILE, HALF)
        for slot in range(1, LAYERS):
            total = total + z_parts[slot]
        z_sum[...] = total
        for copy in spread():
            copy.start()
        tail[pl.ds(c, 1), pl.ds(sub, 1)] = total.reshape(1, 1, TILE, HALF)

    for j in range(GROUPS):
        target, copy = to_owner(j)

        @pl.when(target != z)
        def _():
            copy.wait_send()

    for s in range(GROUPS):
        source = lax.rem(GROUPS * z + s, CHIPS)
        for core in range(2):

            @pl.when((source != me) | (c != core))
            def _():
                pltpu.make_async_remote_copy(
                    z_sum, tail.at[core, s], t_send.at[0], t_recv.at[core, s],
                    device_id=other, device_id_type=MESH,
                ).wait_recv()

    @pl.when(owner)
    def _():
        for copy in spread():
            copy.wait_send()

    for half in range(2):
        grad_ref[:, half * HALF : (half + 1) * HALF] = tail[half].reshape(GROUPS * TILE, HALF)


def body(queries, key_rows, value_rows, step_rates, cotangent, fast_init):
    vmem = lambda *shape: pltpu.VMEM(shape, F32)
    half = lambda *shape: pltpu.VMEM(shape, BF16)
    dma = lambda *shape: pltpu.SemaphoreType.DMA(shape)
    any_spec = pl.BlockSpec(memory_space=pl.ANY)
    vmem_spec = pl.BlockSpec(memory_space=pltpu.VMEM)
    return pl.pallas_call(
        kernel,
        out_shape=(
            jax.ShapeDtypeStruct(queries.shape, BF16),
            jax.ShapeDtypeStruct(fast_init.shape, F32),
        ),
        in_specs=[any_spec] * 5 + [vmem_spec],
        out_specs=(vmem_spec, vmem_spec),
        scratch_shapes=[
            half(4, TOKENS, WIDTH),
            vmem(4, TOKENS, WIDTH),
            vmem(4, TOKENS, WIDTH),
            half(4, BOTH, WIDTH),
            half(4, WIDTH, BOTH),
            vmem(1, TOKENS),
            vmem(1, TOKENS),
            vmem(TILE, BOTH),
            vmem(GROUPS, TILE, HALF),
            vmem(GROUPS, CHIPS, TILE, HALF),
            vmem(GROUPS, CHIPS, TILE, HALF),
            vmem(NPEERS, GROUPS, TILE, HALF),
            vmem(GROUPS, TILE, HALF),
            vmem(GROUPS, CHIPS, TILE, HALF),
            vmem(5, PIPES, OWNED, CHIPS, TILE, HALF),
            vmem(PIPES, OWNED, CHIPS, TILE, HALF),
            vmem(PIPES, NPEERS, OWNED, TILE, HALF),
            vmem(PIPES, OWNED, TILE, HALF),
            half(4 * UNITS, WIDTH),
            half(2 * UNITS, WIDTH),
            vmem(PIPES, UNITS, BOTH),
            vmem(PIPES, UNITS, BOTH),
            vmem(PIPES, UNITS, BOTH),
            vmem(2, PIPES, UNITS, BOTH),
            vmem(2, PIPES, UNITS, BOTH),
            vmem(2, PIPES, UNITS, BOTH),
            vmem(2, PIPES, UNITS, BOTH),
            half(4 * UNITS, BOTH),
            half(PIPES, 2 * UNITS, BOTH),
            vmem(TOKENS, WIDTH),
            vmem(TOKENS, WIDTH),
            vmem(TOKENS, WIDTH),
            vmem(LAYERS, TILE, HALF),
            vmem(TILE, HALF),
            vmem(2, GROUPS, TILE, HALF),
            dma(5),
            dma(4), dma(4),
            pltpu.SemaphoreType.DMA, pltpu.SemaphoreType.DMA,
            pltpu.SemaphoreType.DMA, pltpu.SemaphoreType.DMA,
            dma(NPEERS), dma(NPEERS),
            dma(PIPES, NPEERS), dma(PIPES, NPEERS),
            dma(PIPES, NPEERS), dma(PIPES, NPEERS),
            dma(len(Z_STEPS)), dma(GROUPS), dma(GROUPS),
            dma(GROUPS), dma(LAYERS),
            dma(2 * NPEERS + 1), dma(2, GROUPS),
        ],
        compiler_params=pltpu.CompilerParams(
            collective_id=0, has_side_effects=True, vmem_limit_bytes=56 * 2**20
        ),
    )(queries, key_rows, value_rows, step_rates, cotangent, fast_init)


def solution(mesh):
    torus = Mesh(
        mesh.devices.reshape(SIDE, SIDE, 2, mesh.shape["batch"]), ("x", "y", "c", "z")
    )
    return jax.shard_map(
        body,
        mesh=torus,
        in_specs=(
            P("z", SEQ, None),
            P("z", SEQ, None),
            P("z", SEQ, None),
            P("z", SEQ),
            P("z", SEQ, None),
            P("z", None),
        ),
        out_specs=(P("z", SEQ, None), P("z", None)),
        check_vma=False,
    )
```

time: 115 us -> 105 us (0.913)
  Pallas kernels: 112 us -> 102 us
    pallas_call x1, Pallas kernels: 112 us -> 102 us  [body(): pl.pallas_call(kernel, out_shape=(jax.ShapeDtypeStruct(queries.shape, BF1...]
where the time goes in v2:
time: 105 us
  Pallas kernels  102 us (97%)
  local copies, waits for them, and re-layouts  2.31 us (2%)
    pallas_call x1, Pallas kernels, body(): pl.pallas_call(kernel, out_shape=(jax.ShapeDtypeStruct(queries.shape, BF1...  102 us
    unnamed x4, local copies, waits for them, and re-layouts  2.31 us

profile of v2, /device:TPU:1, one launch (start us, length us, event | category | flops | bytes accessed | tf_op | source)
XLA Modules:
  0.0 104.9 jit_solution(8252791723754746137)
XLA Ops:
  0.6 101.9 %shard_map.77 = (bf16[1,512,256]{2,1,0:T(8,128)(2,1)}, f32[48,256]{1,0:T(8,128)}) custom-call(bf16[1,512,256]{2,1,0:T(8,128)(2,1)} %q_in.1, bf16[1,512,256]{2,1,0:T(8,128)(2,1)} %k_in.1, bf16[1,512,256]{2,1,0:T(8,128)(2,1)} %v_in.1, f32[1,512]{1,0:T(1,128)} %rates_in.1, bf16[1,512,256]{2,1,0:T(8,128)(2,1)} %cot_in.1, f32[48,256]{1,0:T(8,128)} %w_in.1), custom_call_target="tpu_custom_call" | custom-call | tf_op jit(solution)/shard_map/pallas_call | solution.py:533
  102.6 0.0 copy-start
  102.6 1.7 %copy.10 = bf16[1,512,256]{2,1,0:T(8,128)(2,1)} copy(bf16[1,512,256]{2,1,0:T(8,128)(2,1)} %get-tuple-element.4) | data formatting | bytes 524288
  104.3 0.0 copy-done
  104.3 0.6 copy.11
Async XLA Ops:
  102.6 1.7 %copy-start = (f32[48,256]{1,0:T(8,128)S(1)}, f32[48,256]{1,0:T(8,128)}, u32[]{:S(2)}) copy-start(f32[48,256]{1,0:T(8,128)} %get-tuple-element.5) | copy-start | bytes 147460

commit v3 on v2

--- a/solution.py
+++ b/solution.py
@@ -58,43 +58,44 @@
     whole, part, parts, chunk,
     lhs_ab, lhs_c,
     pre_p, pre_g, pre_u, c1, c2, c3, c4,
-    d_pair, e_pair, out_own, out_part, out_other, z_parts, z_sum, tail,
+    d_pair, e_pair, out_own, out_part, out_other, z_parts, z_sum, tail, waits, out_final,
     load_sem, x_send, x_recv, r_send, r_recv, o_send, o_recv,
     n_send, n_recv, rs_send, rs_recv, ag_send, ag_recv,
-    z_send, z_recv, zz_send, y_send, y_recv, t_send, t_recv,
+    z_send, z_recv, zz_send, y_send, y_recv, t_send, t_recv, out_sem, grad_sem,
 ):
     x, y, c, z = (lax.axis_index(name) for name in ("x", "y", "c", "z"))
     me = x * SIDE + y
     other = (x, y, 1 - c, z)
+
+    def peer(step):
+        px = lax.rem(x + step[0], SIDE)
+        py = lax.rem(y + step[1], SIDE)
+        return (px, py, c, z), px * SIDE + py
+
+    def z_peer(dz):
+        return (x, y, c, lax.rem(z + dz, LAYERS))
+
+    peers = [peer(step) for step in PEERS]
+    everyone = [(d[0], d[1], core, z) for d, _ in peers for core in (c, 1 - c)] + [other]
+
+    barrier = pltpu.get_barrier_semaphore()
+    greeted = [z_peer(dz) for dz in Z_STEPS] + everyone
+    for device in greeted:
+        pl.semaphore_signal(barrier, inc=1, device_id=device, device_id_type=MESH)
 
     loads = [
         pltpu.make_async_copy(src.at[0], tok.at[i], load_sem.at[i])
         for i, src in enumerate((k_in, v_in, q_in, cot_in))
     ]
     loads.append(pltpu.make_async_copy(rates_in, rates_own, load_sem.at[4]))
+    for half in range(2):
+        @pl.when(c == half)
+        def _():
+            pltpu.make_async_copy(
+                w_in.at[:, :, half * HALF : (half + 1) * HALF], w_own, load_sem.at[5]
+            ).start()
     for load in loads:
         load.start()
-
-    def peer(step):
-        px = lax.rem(x + step[0], SIDE)
-        py = lax.rem(y + step[1], SIDE)
-        return (px, py, c, z), px * SIDE + py
-
-    def z_peer(dz):
-        return (x, y, c, lax.rem(z + dz, LAYERS))
-
-    peers = [peer(step) for step in PEERS]
-    everyone = [(d[0], d[1], core, z) for d, _ in peers for core in (c, 1 - c)] + [other]
-
-    barrier = pltpu.get_barrier_semaphore()
-    greeted = [z_peer(dz) for dz in Z_STEPS] + everyone
-    for device in greeted:
-        pl.semaphore_signal(barrier, inc=1, device_id=device, device_id_type=MESH)
-
-    for half in range(2):
-        @pl.when(c == half)
-        def _():
-            w_own[...] = w_in[:, half * HALF : (half + 1) * HALF].reshape(GROUPS, TILE, HALF)
 
     divisor = math.sqrt(lax.axis_size(SEQ) * TOKENS)
     for load in loads:
@@ -103,6 +104,7 @@
         mine[i] = tok[i].astype(F32)
     eta[:, 0:TOKENS] = jnp.broadcast_to(-(rates_own[...] / divisor), (TILE, TOKENS))
 
+    pltpu.make_async_copy(w_own, w_own, load_sem.at[5]).wait()
     pl.semaphore_wait(barrier, len(greeted))
 
     sub = lax.rem(me + GROUPS * LAYERS - GROUPS * z, CHIPS)
@@ -184,25 +186,31 @@
         def _():
             z_landed(j)
 
+    def pass_round(j):
+        for device, _ in peers:
+            pltpu.make_async_remote_copy(
+                n_chunk.at[j], natural.at[j, me], n_send, n_recv, device_id=device, device_id_type=MESH
+            ).start()
+        natural[j, pl.ds(me, 1)] = n_chunk[pl.ds(j, 1)]
+
+    def far(j):
+        return (z_away(j) > NEAR) & (z_away(j) < LAYERS - NEAR)
+
+    for j in range(GROUPS):
+        @pl.when((z_away(j) <= NEAR) | (z_away(j) >= LAYERS - NEAR))
+        def _():
+            pass_round(j)
+
     for i in range(2):
         other_tokens(i)
     swaps[4].wait()
     eta[:, TOKENS:BOTH] = jnp.broadcast_to(-(rates_other[...] / divisor), (TILE, TOKENS))
 
     for j in range(GROUPS):
-        @pl.when((z_away(j) > NEAR) & (z_away(j) < LAYERS - NEAR))
+        @pl.when(far(j))
         def _():
             z_landed(j)
-
-    firsts = [
-        pltpu.make_async_remote_copy(
-            n_chunk, natural.at[:, me], n_send.at[k], n_recv.at[k], device_id=device, device_id_type=MESH
-        )
-        for k, (device, _) in enumerate(peers)
-    ]
-    for copy in firsts:
-        copy.start()
-    natural[:, pl.ds(me, 1)] = n_chunk[...].reshape(GROUPS, 1, TILE, HALF)
+            pass_round(j)
 
     for i in (2, 3):
         own_tokens(i)
@@ -222,27 +230,29 @@
         def _():
             z_pass(j, -1).wait_send()
 
+    def all_of(landed, semaphore):
+        pltpu.make_async_copy(landed, landed, semaphore).wait()
+
     def gathering(stage, pipe):
         return [
             pltpu.make_async_remote_copy(
-                chunk.at[pipe], whole.at[stage, pipe, :, me], ag_send.at[pipe, k], ag_recv.at[pipe, k],
+                chunk.at[pipe], whole.at[stage, pipe, :, me], ag_send.at[pipe], ag_recv.at[pipe],
                 device_id=device, device_id_type=MESH,
             )
-            for k, (device, _) in enumerate(peers)
+            for device, _ in peers
         ]
 
     def scattering(pipe):
         return [
             pltpu.make_async_remote_copy(
-                part.at[pipe, :, chip], parts.at[pipe, k], rs_send.at[pipe, k], rs_recv.at[pipe, k],
+                part.at[pipe, :, chip], parts.at[pipe, k], rs_send.at[pipe], rs_recv.at[pipe],
                 device_id=device, device_id_type=MESH,
             )
             for k, (device, chip) in enumerate(peers)
         ]
 
     def reduced(pipe):
-        for copy in scattering(pipe):
-            copy.wait()
+        all_of(parts.at[pipe], rs_recv.at[pipe])
         total = part[pipe, :, pl.ds(me, 1)].reshape(OWNED, TILE, HALF)
         for k in range(NPEERS):
             total = total + parts[pipe, k]
@@ -253,10 +263,11 @@
         for copy in gathering(stage, pipe):
             copy.start()
         whole[stage, pipe, :, pl.ds(me, 1)] = value.reshape(OWNED, 1, TILE, HALF)
+        all_of(parts.at[pipe], rs_send.at[pipe])
 
     def gathered(stage, pipe):
-        for copy in gathering(stage, pipe):
-            copy.wait()
+        all_of(whole.at[stage, pipe, :, pl.ds(0, NPEERS)], ag_recv.at[pipe])
+        all_of(parts.at[pipe], ag_send.at[pipe])
 
     def from_tiles(tiles):
         flat = tiles.reshape(TILES, TILE, HALF)
@@ -371,8 +382,8 @@
         token_loop(body)
         return contract(0, 1, pipe)
 
-    for copy in firsts:
-        copy.wait()
+    all_of(natural.at[:, pl.ds(0, NPEERS)], n_recv)
+    all_of(n_parts, n_send)
     flipped = [
         natural[2 * i : 2 * i + 2].reshape(WIDTH, HALF).T for i in range(3)
     ]
@@ -420,7 +431,9 @@
     for pipe in range(PIPES):
         gather(3, pipe, reduced(pipe))
     swap.wait()
-    out_ref[0] = (out_own[...] + out_other[...]).astype(BF16)
+    out_final[...] = (out_own[...] + out_other[...]).astype(BF16)
+    out_copy = pltpu.make_async_copy(out_final, out_ref.at[0], out_sem)
+    out_copy.start()
 
     for pipe in range(PIPES):
         gathered(3, pipe)
@@ -442,7 +455,7 @@
         n_part[2 * i : 2 * i + 2] = value
     lasts = [
         pltpu.make_async_remote_copy(
-            n_part.at[:, chip], n_parts.at[k], n_send.at[k], n_recv.at[k],
+            n_part.at[:, chip], n_parts.at[k], n_send, n_recv,
             device_id=device, device_id_type=MESH,
         )
         for k, (device, chip) in enumerate(peers)
@@ -452,8 +465,7 @@
     for i, value in enumerate(upright([from_tiles(whole[4, pipe]) for pipe in range(PIPES)])):
         n_adj[2 * i : 2 * i + 2] = value
     total = (n_adj[:, pl.ds(me, 1)] - n_part[:, pl.ds(me, 1)]).reshape(GROUPS, TILE, HALF)
-    for copy in lasts:
-        copy.wait()
+    all_of(n_parts, n_recv)
     for k in range(NPEERS):
         total = total - n_parts[k]
     n_chunk[...] = total
@@ -462,7 +474,7 @@
         target = lax.div(CHIPS * j + me, GROUPS)
         slot = lax.rem(target + LAYERS - z, LAYERS)
         return target, pltpu.make_async_remote_copy(
-            n_chunk.at[j], z_parts.at[slot], y_send.at[j], y_recv.at[slot],
+            n_chunk.at[j], z_parts.at[slot - 1], y_send.at[j], y_recv,
             device_id=(x, y, c, target), device_id_type=MESH,
         )
 
@@ -472,25 +484,25 @@
         @pl.when(target != z)
         def _():
             copy.start()
+
+    spread_bytes = waits.at[0 : len(everyone)]
+
+    all_of(n_parts, n_send)
 
     def spread():
         return [
             pltpu.make_async_remote_copy(
-                z_sum, tail.at[c, sub], t_send.at[k], t_recv.at[c, sub],
+                z_sum, tail.at[c, sub], t_send, t_recv.at[c, sub],
                 device_id=device, device_id_type=MESH,
             )
-            for k, device in enumerate(everyone)
+            for device in everyone
         ]
 
     @pl.when(owner)
     def _():
-        for slot in range(1, LAYERS):
-            pltpu.make_async_remote_copy(
-                n_chunk.at[0], z_parts.at[slot], y_send.at[0], y_recv.at[slot],
-                device_id=other, device_id_type=MESH,
-            ).wait_recv()
+        all_of(z_parts, y_recv)
         total = n_chunk[pl.ds(at, 1)].reshape(TILE, HALF)
-        for slot in range(1, LAYERS):
+        for slot in range(LAYERS - 1):
             total = total + z_parts[slot]
         z_sum[...] = total
         for copy in spread():
@@ -511,32 +523,40 @@
             @pl.when((source != me) | (c != core))
             def _():
                 pltpu.make_async_remote_copy(
-                    z_sum, tail.at[core, s], t_send.at[0], t_recv.at[core, s],
+                    z_sum, tail.at[core, s], t_send, t_recv.at[core, s],
                     device_id=other, device_id_type=MESH,
                 ).wait_recv()
 
     @pl.when(owner)
     def _():
-        for copy in spread():
-            copy.wait_send()
-
-    for half in range(2):
-        grad_ref[:, half * HALF : (half + 1) * HALF] = tail[half].reshape(GROUPS * TILE, HALF)
+        all_of(spread_bytes, t_send)
+
+    grad_copies = [
+        pltpu.make_async_copy(
+            tail.at[half], grad_ref.at[:, :, half * HALF : (half + 1) * HALF], grad_sem.at[half]
+        )
+        for half in range(2)
+    ]
+    for copy in grad_copies:
+        copy.start()
+    out_copy.wait()
+    for copy in grad_copies:
+        copy.wait()
 
 
 def body(queries, key_rows, value_rows, step_rates, cotangent, fast_init):
     vmem = lambda *shape: pltpu.VMEM(shape, F32)
     half = lambda *shape: pltpu.VMEM(shape, BF16)
     dma = lambda *shape: pltpu.SemaphoreType.DMA(shape)
+    vmem_spec = pl.BlockSpec(memory_space=pltpu.VMEM)
     any_spec = pl.BlockSpec(memory_space=pl.ANY)
-    vmem_spec = pl.BlockSpec(memory_space=pltpu.VMEM)
-    return pl.pallas_call(
+    result, grad = pl.pallas_call(
         kernel,
         out_shape=(
-            jax.ShapeDtypeStruct(queries.shape, BF16),
-            jax.ShapeDtypeStruct(fast_init.shape, F32),
+            pltpu.VMEM(queries.shape, BF16),
+            pltpu.VMEM((GROUPS, TILE, WIDTH), F32),
         ),
-        in_specs=[any_spec] * 5 + [vmem_spec],
+        in_specs=[any_spec] * 6,
         out_specs=(vmem_spec, vmem_spec),
         scratch_shapes=[
             half(4, TOKENS, WIDTH),
@@ -571,24 +591,28 @@
             vmem(TOKENS, WIDTH),
             vmem(TOKENS, WIDTH),
             vmem(TOKENS, WIDTH),
-            vmem(LAYERS, TILE, HALF),
+            vmem(LAYERS - 1, TILE, HALF),
             vmem(TILE, HALF),
             vmem(2, GROUPS, TILE, HALF),
-            dma(5),
+            vmem(2 * CHIPS, TILE, HALF),
+            half(TOKENS, WIDTH),
+            dma(6),
             dma(4), dma(4),
             pltpu.SemaphoreType.DMA, pltpu.SemaphoreType.DMA,
             pltpu.SemaphoreType.DMA, pltpu.SemaphoreType.DMA,
-            dma(NPEERS), dma(NPEERS),
-            dma(PIPES, NPEERS), dma(PIPES, NPEERS),
-            dma(PIPES, NPEERS), dma(PIPES, NPEERS),
+            pltpu.SemaphoreType.DMA, pltpu.SemaphoreType.DMA,
+            dma(PIPES), dma(PIPES),
+            dma(PIPES), dma(PIPES),
             dma(len(Z_STEPS)), dma(GROUPS), dma(GROUPS),
-            dma(GROUPS), dma(LAYERS),
-            dma(2 * NPEERS + 1), dma(2, GROUPS),
+            dma(GROUPS), pltpu.SemaphoreType.DMA,
+            pltpu.SemaphoreType.DMA, dma(2, GROUPS),
+            pltpu.SemaphoreType.DMA, dma(2),
         ],
         compiler_params=pltpu.CompilerParams(
             collective_id=0, has_side_effects=True, vmem_limit_bytes=56 * 2**20
         ),
-    )(queries, key_rows, value_rows, step_rates, cotangent, fast_init)
+    )(queries, key_rows, value_rows, step_rates, cotangent, fast_init.reshape(GROUPS, TILE, WIDTH))
+    return result, grad.reshape(fast_init.shape)
 
 
 def solution(mesh):

time: 105 us -> 98.4 us (0.937)
  Pallas kernels: 102 us -> 96.3 us
    pallas_call x1, Pallas kernels: 102 us -> 96.3 us  [body(): pl.pallas_call(kernel, out_shape=(pltpu.VMEM(queries.shape, BF16), pltpu....]
    unnamed x4 -> x2, local copies, waits for them, and re-layouts: 2.31 us -> 1.32 us
where the time goes in v3:
time: 98.4 us; the launch traced here: 98.3 us
  Pallas kernels  96.3 us (98%)
  local copies, waits for them, and re-layouts  1.32 us (1%)
    pallas_call x1, Pallas kernels, body(): pl.pallas_call(kernel, out_shape=(pltpu.VMEM(queries.shape, BF16), pltpu....  96.3 us

profile of v3, /device:TPU:1, one launch (start us, length us, event | category | flops | bytes accessed | tf_op | source)
XLA Modules:
  0.0 98.3 jit_solution(17264918357294344122)
XLA Ops:
  0.6 96.3 %shard_map.77 = (bf16[1,512,256]{2,1,0:T(8,128)(2,1)S(1)}, f32[6,8,256]{2,1,0:T(8,128)S(1)}) custom-call(bf16[1,512,256]{2,1,0:T(8,128)(2,1)} %q_in.1, bf16[1,512,256]{2,1,0:T(8,128)(2,1)} %k_in.1, bf16[1,512,256]{2,1,0:T(8,128)(2,1)} %v_in.1, f32[1,512]{1,0:T(1,128)} %rates_in.1, bf16[1,512,256]{2,1,0:T(8,128)(2,1)} %cot_in.1, f32[6,8,256]{2,1,0:T(8,128)} %bitcast.3), custom_call_target="tpu_custom_call" | custom-call | tf_op jit(solution)/shard_map/pallas_call | solution.py:553
  97.0 0.7 copy.10
  97.7 0.6 copy.11

commit v4 on v3

--- a/solution.py
+++ b/solution.py
@@ -27,6 +27,8 @@
 HEIGHT = 3 * UNITS
 TILES = 2 * HEIGHT // TILE
 OWNED = TILES // CHIPS
+STRIP = GROUPS * TILE // PIPES
+SHARE = STRIP // TILE
 NEAR = 4
 
 
@@ -54,14 +56,14 @@
     q_in, k_in, v_in, rates_in, cot_in, w_in,
     out_ref, grad_ref,
     tok, mine, theirs, tok_b, tok_t, rates_own, rates_other, eta, w_own,
-    natural, n_part, n_parts, n_chunk, n_adj,
+    natural, n_chunk, adj,
     whole, part, parts, chunk,
     lhs_ab, lhs_c,
     pre_p, pre_g, pre_u, c1, c2, c3, c4,
-    d_pair, e_pair, out_own, out_part, out_other, z_parts, z_sum, tail, waits, out_final,
+    d_pair, e_pair, out_own, out_part, out_other, z_parts, z_sum, tail, waits,
     load_sem, x_send, x_recv, r_send, r_recv, o_send, o_recv,
     n_send, n_recv, rs_send, rs_recv, ag_send, ag_recv,
-    z_send, z_recv, zz_send, y_send, y_recv, t_send, t_recv, out_sem, grad_sem,
+    z_send, z_recv, zz_send, y_send, y_recv, t_send, t_recv,
 ):
     x, y, c, z = (lax.axis_index(name) for name in ("x", "y", "c", "z"))
     me = x * SIDE + y
@@ -383,7 +385,7 @@
         return contract(0, 1, pipe)
 
     all_of(natural.at[:, pl.ds(0, NPEERS)], n_recv)
-    all_of(n_parts, n_send)
+    all_of(natural.at[:, pl.ds(0, NPEERS)], n_send)
     flipped = [
         natural[2 * i : 2 * i + 2].reshape(WIDTH, HALF).T for i in range(3)
     ]
@@ -431,9 +433,7 @@
     for pipe in range(PIPES):
         gather(3, pipe, reduced(pipe))
     swap.wait()
-    out_final[...] = (out_own[...] + out_other[...]).astype(BF16)
-    out_copy = pltpu.make_async_copy(out_final, out_ref.at[0], out_sem)
-    out_copy.start()
+    out_ref[0] = (out_own[...] + out_other[...]).astype(BF16)
 
     for pipe in range(PIPES):
         gathered(3, pipe)
@@ -441,83 +441,79 @@
     for pipe in range(PIPES):
         gather(4, pipe, mine_of(3, pipe) - reduced(pipe))
 
-    def upright(values):
+    first_half = lax.broadcasted_iota(jnp.int32, (LAYERS, STRIP, HALF), 2) < UNITS
+
+    def upright(value):
+        turned = []
         for i in range(3):
-            rows = slice(i * UNITS, (i + 1) * UNITS)
-            matrix = jnp.concatenate([value[rows] for value in values], axis=0)
-            yield matrix.T.reshape(2, CHIPS, TILE, HALF)
-
-    terms = []
+            matrix = value[i * UNITS : (i + 1) * UNITS]
+            turned.append(jnp.concatenate([matrix, matrix], axis=0).T)
+        blocks = jnp.concatenate(turned, axis=0).reshape(LAYERS, 2, STRIP, HALF)
+        packed = jnp.where(first_half, blocks[:, 0], blocks[:, 1])
+        return packed.reshape(OWNED, CHIPS, TILE, HALF)
+
     for pipe in range(PIPES):
         gathered(4, pipe)
-        terms.append(hessian(0, 4, pipe))
-    for i, value in enumerate(upright(terms)):
-        n_part[2 * i : 2 * i + 2] = value
-    lasts = [
-        pltpu.make_async_remote_copy(
-            n_part.at[:, chip], n_parts.at[k], n_send, n_recv,
-            device_id=device, device_id_type=MESH,
-        )
-        for k, (device, chip) in enumerate(peers)
-    ]
-    for copy in lasts:
-        copy.start()
-    for i, value in enumerate(upright([from_tiles(whole[4, pipe]) for pipe in range(PIPES)])):
-        n_adj[2 * i : 2 * i + 2] = value
-    total = (n_adj[:, pl.ds(me, 1)] - n_part[:, pl.ds(me, 1)]).reshape(GROUPS, TILE, HALF)
-    all_of(n_parts, n_recv)
-    for k in range(NPEERS):
-        total = total - n_parts[k]
-    n_chunk[...] = total
-
-    def to_owner(j):
-        target = lax.div(CHIPS * j + me, GROUPS)
+        part[pipe] = upright(hessian(0, 4, pipe))
+        for copy in scattering(pipe):
+            copy.start()
+
+    last_sub = lax.rem(me + SHARE * LAYERS - SHARE * z, CHIPS)
+    last_at = lax.div(SHARE * z + last_sub, CHIPS)
+    last_owner = last_sub < SHARE
+
+    def to_owner(pipe, j):
+        target = lax.div(CHIPS * j + me, SHARE)
         slot = lax.rem(target + LAYERS - z, LAYERS)
         return target, pltpu.make_async_remote_copy(
-            n_chunk.at[j], z_parts.at[slot - 1], y_send.at[j], y_recv,
+            chunk.at[pipe, j], z_parts.at[pipe, slot - 1], y_send.at[pipe, j], y_recv.at[pipe],
             device_id=(x, y, c, target), device_id_type=MESH,
         )
 
-    for j in range(GROUPS):
-        target, copy = to_owner(j)
-
-        @pl.when(target != z)
-        def _():
-            copy.start()
-
-    spread_bytes = waits.at[0 : len(everyone)]
-
-    all_of(n_parts, n_send)
+    for pipe in range(PIPES):
+        adj[pipe] = upright(from_tiles(whole[4, pipe]))
+    for pipe in range(PIPES):
+        chunk[pipe] = adj[pipe, :, pl.ds(me, 1)].reshape(OWNED, TILE, HALF) - reduced(pipe)
+        for j in range(OWNED):
+            target, copy = to_owner(pipe, j)
+
+            @pl.when(target != z)
+            def _():
+                copy.start()
+
+        all_of(parts.at[pipe], rs_send.at[pipe])
 
     def spread():
         return [
             pltpu.make_async_remote_copy(
-                z_sum, tail.at[c, sub], t_send, t_recv.at[c, sub],
+                z_sum, tail.at[c, last_sub], t_send, t_recv.at[c, last_sub],
                 device_id=device, device_id_type=MESH,
             )
             for device in everyone
         ]
 
-    @pl.when(owner)
+    @pl.when(last_owner)
     def _():
-        all_of(z_parts, y_recv)
-        total = n_chunk[pl.ds(at, 1)].reshape(TILE, HALF)
-        for slot in range(LAYERS - 1):
-            total = total + z_parts[slot]
-        z_sum[...] = total
+        for pipe in range(PIPES):
+            all_of(z_parts.at[pipe], y_recv.at[pipe])
+            total = chunk[pipe, pl.ds(last_at, 1)].reshape(TILE, HALF)
+            for slot in range(LAYERS - 1):
+                total = total + z_parts[pipe, slot]
+            z_sum[pipe] = total
         for copy in spread():
             copy.start()
-        tail[pl.ds(c, 1), pl.ds(sub, 1)] = total.reshape(1, 1, TILE, HALF)
-
-    for j in range(GROUPS):
-        target, copy = to_owner(j)
-
-        @pl.when(target != z)
-        def _():
-            copy.wait_send()
-
-    for s in range(GROUPS):
-        source = lax.rem(GROUPS * z + s, CHIPS)
+        tail[pl.ds(c, 1), pl.ds(last_sub, 1)] = z_sum[...].reshape(1, 1, PIPES, TILE, HALF)
+
+    for pipe in range(PIPES):
+        for j in range(OWNED):
+            target, copy = to_owner(pipe, j)
+
+            @pl.when(target != z)
+            def _():
+                copy.wait_send()
+
+    for s in range(SHARE):
+        source = lax.rem(SHARE * z + s, CHIPS)
         for core in range(2):
 
             @pl.when((source != me) | (c != core))
@@ -527,21 +523,17 @@
                     device_id=other, device_id_type=MESH,
                 ).wait_recv()
 
-    @pl.when(owner)
+    low = lax.broadcasted_iota(jnp.int32, (TILE, HALF), 1) < UNITS
+    for core in range(2):
+        for s in range(SHARE):
+            one, two = tail[core, s, 0], tail[core, s, 1]
+            cols = slice(core * HALF, (core + 1) * HALF)
+            grad_ref[s, :, cols] = jnp.where(low, one, pltpu.roll(two, UNITS, 1))
+            grad_ref[SHARE + s, :, cols] = jnp.where(low, pltpu.roll(one, UNITS, 1), two)
+
+    @pl.when(last_owner)
     def _():
-        all_of(spread_bytes, t_send)
-
-    grad_copies = [
-        pltpu.make_async_copy(
-            tail.at[half], grad_ref.at[:, :, half * HALF : (half + 1) * HALF], grad_sem.at[half]
-        )
-        for half in range(2)
-    ]
-    for copy in grad_copies:
-        copy.start()
-    out_copy.wait()
-    for copy in grad_copies:
-        copy.wait()
+        all_of(waits, t_send)
 
 
 def body(queries, key_rows, value_rows, step_rates, cotangent, fast_init):
@@ -569,10 +561,8 @@
             vmem(TILE, BOTH),
             vmem(GROUPS, TILE, HALF),
             vmem(GROUPS, CHIPS, TILE, HALF),
-            vmem(GROUPS, CHIPS, TILE, HALF),
-            vmem(NPEERS, GROUPS, TILE, HALF),
             vmem(GROUPS, TILE, HALF),
-            vmem(GROUPS, CHIPS, TILE, HALF),
+            vmem(PIPES, OWNED, CHIPS, TILE, HALF),
             vmem(5, PIPES, OWNED, CHIPS, TILE, HALF),
             vmem(PIPES, OWNED, CHIPS, TILE, HALF),
             vmem(PIPES, NPEERS, OWNED, TILE, HALF),
@@ -591,11 +581,10 @@
             vmem(TOKENS, WIDTH),
             vmem(TOKENS, WIDTH),
             vmem(TOKENS, WIDTH),
-            vmem(LAYERS - 1, TILE, HALF),
-            vmem(TILE, HALF),
-            vmem(2, GROUPS, TILE, HALF),
-            vmem(2 * CHIPS, TILE, HALF),
-            half(TOKENS, WIDTH),
+            vmem(PIPES, LAYERS - 1, TILE, HALF),
+            vmem(PIPES, TILE, HALF),
+            vmem(2, SHARE, PIPES, TILE, HALF),
+            vmem(2 * NPEERS + 1, PIPES, TILE, HALF),
             dma(6),
             dma(4), dma(4),
             pltpu.SemaphoreType.DMA, pltpu.SemaphoreType.DMA,
@@ -604,9 +593,8 @@
             dma(PIPES), dma(PIPES),
             dma(PIPES), dma(PIPES),
             dma(len(Z_STEPS)), dma(GROUPS), dma(GROUPS),
-            dma(GROUPS), pltpu.SemaphoreType.DMA,
-            pltpu.SemaphoreType.DMA, dma(2, GROUPS),
-            pltpu.SemaphoreType.DMA, dma(2),
+            dma(PIPES, OWNED), dma(PIPES),
+            pltpu.SemaphoreType.DMA, dma(2, SHARE),
         ],
         compiler_params=pltpu.CompilerParams(
             collective_id=0, has_side_effects=True, vmem_limit_bytes=56 * 2**20

time: 98.4 us -> 96.7 us (0.983)
  Pallas kernels: 96.3 us -> 94.6 us
    pallas_call x1, Pallas kernels: 96.3 us -> 94.6 us  [body(): pl.pallas_call(kernel, out_shape=(pltpu.VMEM(queries.shape, BF16), pltpu....]
where the time goes in v4:
time: 96.7 us; the launch traced here: 96.6 us
  Pallas kernels  94.6 us (98%)
  local copies, waits for them, and re-layouts  1.32 us (1%)
    pallas_call x1, Pallas kernels, body(): pl.pallas_call(kernel, out_shape=(pltpu.VMEM(queries.shape, BF16), pltpu....  94.6 us

profile of v4, /device:TPU:1, one launch (start us, length us, event | category | flops | bytes accessed | tf_op | source)
XLA Modules:
  0.0 96.6 jit_solution(15738939391924040891)
XLA Ops:
  0.6 94.6 %shard_map.77 = (bf16[1,512,256]{2,1,0:T(8,128)(2,1)S(1)}, f32[6,8,256]{2,1,0:T(8,128)S(1)}) custom-call(bf16[1,512,256]{2,1,0:T(8,128)(2,1)} %q_in.1, bf16[1,512,256]{2,1,0:T(8,128)(2,1)} %k_in.1, bf16[1,512,256]{2,1,0:T(8,128)(2,1)} %v_in.1, f32[1,512]{1,0:T(1,128)} %rates_in.1, bf16[1,512,256]{2,1,0:T(8,128)(2,1)} %cot_in.1, f32[6,8,256]{2,1,0:T(8,128)} %bitcast.3), custom_call_target="tpu_custom_call" | custom-call | tf_op jit(solution)/shard_map/pallas_call | solution.py:545
  95.3 0.7 copy.10
  96.0 0.6 copy.11

commit v5 on v4

--- a/solution.py
+++ b/solution.py
@@ -392,12 +392,11 @@
     for pipe in range(PIPES):
         rows = slice(pipe * UNITS, (pipe + 1) * UNITS)
         whole[0, pipe] = to_tiles(jnp.concatenate([matrix[rows] for matrix in flipped], axis=0))
+        scatter(pipe, inner(0, pipe))
 
     def mine_of(stage, pipe):
         return whole[stage, pipe, :, pl.ds(me, 1)].reshape(OWNED, TILE, HALF)
 
-    for pipe in range(PIPES):
-        scatter(pipe, inner(0, pipe))
     for pipe in range(PIPES):
         inner_second(0, pipe)
     for pipe in range(PIPES):
@@ -534,6 +533,17 @@
     @pl.when(last_owner)
     def _():
         all_of(waits, t_send)
+
+
+def hand_over(out_in, grad_in, out_ref, grad_ref, sems):
+    copies = [
+        pltpu.make_async_copy(grad_in, grad_ref, sems.at[0]),
+        pltpu.make_async_copy(out_in, out_ref, sems.at[1]),
+    ]
+    for copy in copies:
+        copy.start()
+    for copy in copies:
+        copy.wait()
 
 
 def body(queries, key_rows, value_rows, step_rates, cotangent, fast_init):
@@ -600,6 +610,18 @@
             collective_id=0, has_side_effects=True, vmem_limit_bytes=56 * 2**20
         ),
     )(queries, key_rows, value_rows, step_rates, cotangent, fast_init.reshape(GROUPS, TILE, WIDTH))
+    result = pltpu.with_memory_space_constraint(result, pltpu.VMEM)
+    grad = pltpu.with_memory_space_constraint(grad, pltpu.VMEM)
+    result, grad = pl.pallas_call(
+        hand_over,
+        out_shape=(
+            jax.ShapeDtypeStruct(queries.shape, BF16),
+            jax.ShapeDtypeStruct((GROUPS, TILE, WIDTH), F32),
+        ),
+        in_specs=[vmem_spec] * 2,
+        out_specs=(any_spec,) * 2,
+        scratch_shapes=[dma(2)],
+    )(result, grad)
     return result, grad.reshape(fast_init.shape)
 
 

time: 96.7 us -> 96 us (level)
  local copies, waits for them, and re-layouts: 1.32 us -> 0 us
    unnamed x2 -> x0, local copies, waits for them, and re-layouts: 1.32 us -> none
where the time goes in v5:
time: 96 us; the launch traced here: 95.9 us
  Pallas kernels  95.2 us (99%)
    pallas_call x1, Pallas kernels, body(): pl.pallas_call(kernel, out_shape=(pltpu.VMEM(queries.shape, BF16), pltpu....  94.5 us

profile of v5, /device:TPU:1, one launch (start us, length us, event | category | flops | bytes accessed | tf_op | source)
XLA Modules:
  0.0 95.9 jit_solution(3904865263077871400)
XLA Ops:
  0.6 94.5 %shard_map.77 = (bf16[1,512,256]{2,1,0:T(8,128)(2,1)S(1)}, f32[6,8,256]{2,1,0:T(8,128)S(1)}) custom-call(bf16[1,512,256]{2,1,0:T(8,128)(2,1)} %q_in.1, bf16[1,512,256]{2,1,0:T(8,128)(2,1)} %k_in.1, bf16[1,512,256]{2,1,0:T(8,128)(2,1)} %v_in.1, f32[1,512]{1,0:T(1,128)} %rates_in.1, bf16[1,512,256]{2,1,0:T(8,128)(2,1)} %cot_in.1, f32[6,8,256]{2,1,0:T(8,128)} %bitcast.2), custom_call_target="tpu_custom_call" | custom-call | tf_op jit(solution)/shard_map/pallas_call | solution.py:555
  95.1 0.7 shard_map.78
